TPU v7x, 32 devices: a whole 2x2x4 slice. The times are simulated.
32 devices in a mesh: grp: 2 (over y), lon: 4 (over z), lat: 2 (over x), dir: 2 (over core).
Axes of the slice: x: 2, y: 2, z: 4, core: 2. Of those that a mesh axis runs over, the one named last changes fastest.
Arguments:
- perturb: float32 [6, 16, 64, 512], P('grp', 'dir', 'lat', 'lon'), parts along dimension 0, may hold values from -6 to 6
- background: float32 [6, 64, 512], P('grp', 'lat', 'lon'), parts along dimension 0, may hold values from -0.3 to 0.3
- land_mask: int32 [64, 512], P('lat', 'lon'), may hold values 0 or 1
- levels: int32 [64, 512], P('lat', 'lon'), may hold values from 1 to 90
- fold_partner: int32 [512], replicated, may hold values from 0 to 511, as said below
Outputs:
- evolved: float32 [6, 16, 64, 512], P('grp', 'dir', 'lat', 'lon'), parts along dimension 0
There are 2 independent parts, one for each index of `grp`. A program takes and returns all parts, laid end to end along the dimension named above; an argument that names none is the same for every part. Nothing has to cross between parts.
Inputs may be any that keep to these rules, and one draw needn't show every extreme that they name: fold_partner[i] = (P - i) mod 512 for one odd P of the draw.
All inputs are finite; a program needn't handle non-finite values. No bound on the sum of `land_mask` on one device may be relied on, other than what follows from the above.
Results may differ from a plain program's by a relative error of at most 0.00002.
Values sent between devices are 32-bit elements; how exact they have to be, the bound alone decides.
No kernel may reach another device: no remote copies, remote signals or barrier semaphores. Data moves between devices by JAX's collectives and lax.ppermute only.
A program may use at most 64 MiB of HBM per device.

v0:
```python
import functools
from collections import deque

import jax
import jax.numpy as jnp
from jax import lax
from jax.experimental import pallas as pl
from jax.experimental.pallas import tpu as pltpu
from jax.sharding import PartitionSpec as P

SUBCYCLES = 5
NLEV = 90
TIME_STEP = 0.35
HALF_STEP = 0.5 * TIME_STEP

LANES = 128
SUBLANES = 8
HALF = LANES // 2
HALO = 2 * SUBCYCLES
PAIRS = HALO // 2
FIELDS = 4
STATE = 3
COEF = 3
STRIP_SLOTS = HALF // HALO
CORNER_SLOTS = LANES // (2 * HALO)
F32 = jnp.float32


def ceil_div(a, b):
    return -(-a // b)


class Shapes:
    def __init__(self, height):
        self.height = height
        self.ext = height + 2 * HALO
        self.mid = self.ext // 2
        self.fold_first = height
        self.blocks = FIELDS * PAIRS
        self.strip_rows = height // 2
        self.strips = ceil_div(self.strip_rows * FIELDS, STRIP_SLOTS)
        self.side = self.blocks + self.strips
        self.main = STATE * HALO + PAIRS
        self.corners = ceil_div(FIELDS * HALO, CORNER_SLOTS)
        self.band = self.main + self.corners

    def strip(self, k, f):
        slot = (k - HALO) * FIELDS + f
        return self.blocks + slot // STRIP_SLOTS, HALO * (slot % STRIP_SLOTS)

    def corner(self, i, f):
        slot = f * HALO + i
        return self.main + slot // CORNER_SLOTS, 2 * HALO * (slot % CORNER_SLOTS)


def by_register(items, where):
    groups = {}
    for i, f in items:
        v, at = where(i, f)
        groups.setdefault(v, []).append((i, f, at))
    return groups


def roll(x, shift, axis=1):
    shift = shift % x.shape[axis]
    return x if shift == 0 else pltpu.roll(x, shift, axis)


def lane_ids():
    return lax.broadcasted_iota(jnp.int32, (SUBLANES, LANES), 1)


def sublane_ids():
    return lax.broadcasted_iota(jnp.int32, (SUBLANES, LANES), 0)


def run_staged(tasks, window):
    waiting = deque()

    def advance(task):
        try:
            next(task)
        except StopIteration:
            return
        waiting.append(task)

    for task in tasks:
        advance(task)
        while len(waiting) >= window:
            advance(waiting.popleft())
    while waiting:
        advance(waiting.popleft())


def row(ref, f, r):
    return ref[f, SUBLANES * r : SUBLANES * (r + 1), :]


def put_row(ref, f, r, value):
    ref[f, SUBLANES * r : SUBLANES * (r + 1), :] = value


def coef(ref, r, c):
    return jnp.broadcast_to(ref[SUBLANES * r + c : SUBLANES * r + c + 1, :], (SUBLANES, LANES))


def even_lon():
    return jnp.full((SUBLANES, LANES), lax.rem(lax.axis_index("lon"), 2), jnp.int32) == 0


def fold_place(fold_ref, lon_size):
    pivot = fold_ref[0]
    block = pivot // LANES
    rest = pivot - block * LANES
    low = rest < HALF
    place = jnp.where(low, rest + LANES, rest)
    branch = jnp.where(low, block - 1 + lon_size, block)
    return lax.rem(branch, lon_size), place


def pair_coefs(a, b):
    return jnp.where(sublane_ids() < SUBLANES // 2, a, roll(b, SUBLANES // 2, 0))


def sides_kernel(sh, sizes, x_hbm, b_hbm, m_hbm, l_hbm, p_hbm, *rest):
    a_out, b_out, own_ref, place_out, q_out = rest[:5]
    lat_outs, (x_ref, b_ref, m_ref, l_ref, p_ref, sems) = rest[5:-6], rest[-6:]
    lat_size, lon_size = sizes
    height = sh.height
    copies = [
        pltpu.make_async_copy(src, dst, sems.at[n])
        for n, (src, dst) in enumerate(
            [(b_hbm, b_ref), (m_hbm, m_ref), (l_hbm, l_ref), (p_hbm, p_ref)]
            + [(x_hbm.at[f], x_ref.at[f]) for f in range(STATE)]
        )
    ]
    for copy in copies:
        copy.start()
    for copy in copies[:4]:
        copy.wait()
    q_out[0], place = fold_place(p_ref, lon_size)
    place_out[...] = jnp.full((SUBLANES, LANES), place, jnp.int32)

    wet = m_ref[...].astype(F32)
    depth = 0.5 + 1.5 * ((l_ref[...] - 1).astype(F32) / (NLEV - 1)) ** 2
    row0 = lax.axis_index("lat") * height
    rows = (row0 + lax.broadcasted_iota(jnp.int32, (height, LANES), 0)).astype(F32)
    coriolis = 0.3 + 0.2 * rows / (height * lat_size)
    planes = [
        HALF_STEP * (wet * (depth + b_ref[0])),
        HALF_STEP * b_ref[1],
        HALF_STEP * b_ref[2],
        wet * (TIME_STEP * coriolis),
        wet,
    ]
    planes += [jnp.zeros_like(wet)] * (SUBLANES - len(planes))
    for c, plane in enumerate(planes):
        for r in range(0, height, SUBLANES):
            own_ref[COEF, pl.ds(SUBLANES * r + c, SUBLANES, stride=SUBLANES), :] = plane[
                r : r + SUBLANES
            ]
    for copy in copies[4:]:
        copy.wait()
    for f in range(STATE):
        for r in range(height):
            put_row(own_ref, f, r, x_ref[f, pl.ds(r, SUBLANES, stride=height), :])

    even = even_lon()
    lane = lane_ids()
    low = lane < HALF
    own = functools.partial(row, own_ref)
    top = height - HALO

    def block(f, i):
        a, b = own(f, top + i), own(f, top + i + PAIRS)
        a_up, b_up = roll(a, HALF), roll(b, HALF)
        yield
        east = jnp.where(low, a_up, b)
        west = jnp.where(low, a, b_up)
        v = f * PAIRS + i
        a_out[v] = jnp.where(even, east, west)
        b_out[v] = jnp.where(even, west, east)

    slots = {}
    for k in range(HALO, sh.mid):
        for f in range(FIELDS):
            v, at = sh.strip(k, f)
            slots.setdefault(v, []).append((k, f, at))

    def strips(v):
        parts = []
        for k, f, at in slots[v]:
            a, b = own(f, k - HALO), own(f, sh.ext - 1 - k - HALO)
            beyond = HALF if sh.ext - 1 - k >= sh.fold_first else 0
            parts.append(
                (
                    at,
                    roll(a, at - (LANES - HALO)),
                    roll(b, HALF + at - (LANES - HALO) + beyond),
                    roll(a, at),
                    roll(b, HALF + at - beyond),
                )
            )
        yield
        east = west = jnp.zeros((SUBLANES, LANES), F32)
        for at, ea, eb, wa, wb in parts:
            here = (lane >= at) & (lane < at + HALO)
            there = (lane >= HALF + at) & (lane < HALF + at + HALO)
            east = jnp.where(here, ea, jnp.where(there, eb, east))
            west = jnp.where(here, wa, jnp.where(there, wb, west))
        a_out[v] = jnp.where(even, east, west)
        b_out[v] = jnp.where(even, west, east)

    run_staged([block(f, i) for f in range(FIELDS) for i in range(PAIRS)], 10)
    run_staged([strips(v) for v in sorted(slots)], 2)

    def raw_rows(out, first):
        for f in range(STATE):
            for i in range(HALO):
                out[f * HALO + i] = own(f, first + i)
        for i in range(PAIRS):
            out[STATE * HALO + i] = pair_coefs(
                own(COEF, first + i), own(COEF, first + i + PAIRS)
            )

    lat_even = lax.rem(lax.axis_index("lat"), 2) == 0

    @pl.when(lat_even)
    def _():
        raw_rows(lat_outs[0], top)
        if len(lat_outs) > 1:
            raw_rows(lat_outs[1], 0)

    @pl.when(jnp.logical_not(lat_even))
    def _():
        raw_rows(lat_outs[0], 0)
        if len(lat_outs) > 1:
            raw_rows(lat_outs[1], top)


def bands_kernel(sh, sizes, own_ref, ra_ref, rb_ref, place_ref, fold_out, *lat_outs):
    lat_size, _ = sizes
    even = even_lon()
    lane, sub = lane_ids(), sublane_ids()
    low = lane < HALF
    own = functools.partial(row, own_ref)
    top = sh.height - HALO

    def from_east(v):
        return jnp.where(even, ra_ref[v], rb_ref[v])

    def from_west(v):
        return jnp.where(even, rb_ref[v], ra_ref[v])

    def corners(out, is_top):
        def register(v, items):
            parts = []
            for i, f, at in items:
                if is_top:
                    src, h = f * PAIRS + i % PAIRS, HALF * (i // PAIRS)
                    w_at, e_at = h + HALF - HALO, h
                else:
                    src, w_at = sh.strip(HALO + i, f)
                    e_at = w_at
                parts.append(
                    (at, roll(from_west(src), at - w_at), roll(from_east(src), at + HALO - e_at))
                )
            yield
            total = jnp.zeros((SUBLANES, LANES), F32)
            for at, w, e in parts:
                total = jnp.where((lane >= at) & (lane < at + HALO), w, total)
                total = jnp.where((lane >= at + HALO) & (lane < at + 2 * HALO), e, total)
            out[v - sh.main] = total

        groups = by_register([(i, f) for f in range(FIELDS) for i in range(HALO)], sh.corner)
        run_staged([register(v, items) for v, items in groups.items()], 3)

    lat_even = lax.rem(lax.axis_index("lat"), 2) == 0

    @pl.when(lat_even)
    def _():
        corners(lat_outs[0], True)
        if len(lat_outs) > 1:
            corners(lat_outs[1], False)

    @pl.when(jnp.logical_not(lat_even))
    def _():
        corners(lat_outs[0], False)
        if len(lat_outs) > 1:
            corners(lat_outs[1], True)

    @pl.when(lax.axis_index("lat") == lat_size - 1)
    def _():
        where_to = place_ref[...]
        rest = where_to & (LANES - 1)
        eastern = where_to >= LANES
        backwards = (where_to - lane) & (LANES - 1)
        main_own = (eastern & (lane >= rest + 1)) | (jnp.logical_not(eastern) & (lane <= rest))
        upper = (lane >= rest + 1) & (lane <= rest + HALO)
        lower = (lane >= rest + 1 - HALO) & (lane <= rest)
        side_own = (eastern & lower) | (jnp.logical_not(eastern) & upper)
        side_far = (eastern & upper & (lane >= HALF)) | (
            jnp.logical_not(eastern) & lower & (lane < HALF)
        )
        coef_signs = jnp.where((sub == 1) | (sub == 2), -1.0, 1.0).astype(F32)

        def reversed_row(f, i):
            v, h = f * PAIRS + i % PAIRS, i // PAIRS
            w, e = from_west(v), from_east(v)
            if h == 0:
                w = roll(w, HALF)
            else:
                e = roll(e, HALF)
            v, at = sh.strip(sh.ext - 1 - sh.fold_first - i, f)
            far_w = roll(from_west(v), HALF - HALO - HALF - at)
            far_e = roll(from_east(v), -at)
            yield
            both = jnp.where(low, e, w)
            mine = own(f, top + i)
            main = jnp.where(main_own, mine, both)
            side = jnp.where(
                side_own, mine, jnp.where(side_far, jnp.where(low, far_w, far_e), both)
            )
            if f == COEF:
                main, side = main * coef_signs, side * coef_signs
            elif f > 0:
                main, side = -main, -side
            main = jnp.take_along_axis(main, backwards, axis=1)
            side = jnp.take_along_axis(side, backwards, axis=1)
            yield
            j = HALO - 1 - i
            v, at = sh.corner(j, f)
            side = roll(side, at - (LANES - HALO))
            if f < STATE:
                fold_out[f * HALO + j] = main
            elif j < PAIRS:
                v2 = STATE * HALO + j
                fold_out[v2] = jnp.where(sub < SUBLANES // 2, main, fold_out[v2])
            else:
                fold_out[STATE * HALO + j - PAIRS] = roll(main, SUBLANES // 2, 0)
            yield
            here = (lane >= at) & (lane < at + 2 * HALO)
            fold_out[v] = jnp.where(here, side, fold_out[v])

        for v in range(STATE * HALO, sh.band):
            fold_out[v] = jnp.zeros((SUBLANES, LANES), F32)
        run_staged([reversed_row(f, i) for f in range(FIELDS) for i in range(HALO)], 8)


EAST0 = HALF // 2
LAG = 4
WET, NORTH_THICK = 4, 5


def north_sign():
    return jnp.where(lane_ids() < HALF, 1.0, -1.0).astype(F32)


class Sweep:
    def __init__(self, elev, vel, old, coef, put, known=None, mirror=None):
        self.elev_rows, self.vel_rows = elev, vel
        self.old, self.coef, self.put, self.known, self.mirror = old, coef, put, known, mirror
        self.flux_n, self.rolled, self.new, self.slopes = {}, {}, {}, {}
        self.sign = HALF_STEP * north_sign() if mirror is not None else HALF_STEP
        self.first = min(elev[0] - 1, vel[0])
        self.last = (max(elev[1] + 1, vel[1]) if mirror is None else mirror) + 2 * LAG

    def flux(self, r):
        lo, hi = self.elev_rows
        if not lo - 1 <= r <= hi or r == self.mirror:
            return
        eta, merid = self.old(0, r), self.old(2, r)
        thick = self.coef(r, 0)
        thick_n = thick if self.mirror is None else self.coef(r, NORTH_THICK)
        self.flux_n[r] = thick_n * merid + self.coef(r, 2) * eta
        if lo <= r < hi:
            east = thick * self.old(1, r) + self.coef(r, 1) * eta
            self.rolled[r] = (roll(east, -1), roll(east, 1))
        if self.mirror is not None and r == self.mirror - 1:
            self.flux_n[r + 1] = -roll(self.flux_n[r], HALF)

    def elevation(self, r):
        lo, hi = self.elev_rows
        if not lo <= r < hi:
            return
        plus, minus = self.rolled.pop(r)
        change = (plus - minus) + (self.flux_n[r + 1] - self.flux_n[r - 1])
        eta = self.coef(r, WET) * (self.old(0, r) - change)
        self.new[r] = eta
        self.put(0, r, eta)
        if self.mirror is not None and r == self.mirror - 1:
            self.new[r + 1] = roll(eta, HALF)

    def get_new(self, r):
        if r not in self.new:
            self.new[r] = self.known(r)
            if self.vel_rows[0] <= r < self.vel_rows[1]:
                self.put(0, r, self.new[r])
        return self.new[r]

    def slope(self, r):
        if self.vel_rows[0] <= r < self.vel_rows[1]:
            eta = self.get_new(r)
            self.slopes[r] = (roll(eta, -1), roll(eta, 1))

    def velocity(self, r):
        if not self.vel_rows[0] <= r < self.vel_rows[1]:
            return
        plus, minus = self.slopes.pop(r)
        wet, turn = self.coef(r, WET), self.coef(r, 3)
        zonal, merid = self.old(1, r), self.old(2, r)
        zonal = wet * (zonal - HALF_STEP * (plus - minus)) + turn * merid
        slope = self.sign * (self.get_new(r + 1) - self.get_new(r - 1))
        merid = wet * (merid - slope) - turn * zonal
        self.put(1, r, zonal)
        self.put(2, r, merid)

    def advance(self, t):
        self.flux(t)
        self.elevation(t - LAG)
        self.slope(t - LAG)
        self.velocity(t - 2 * LAG)


def run_sweeps(sweeps):
    for t in range(max(s.last - s.first for s in sweeps) + 1):
        for s in sweeps:
            s.advance(s.first + t)


def middle_kernel(sh, own_ref, hist_ref):
    for step in range(1, SUBCYCLES + 1):
        before, after = hist_ref.at[max(step - 2, 0)], hist_ref.at[step - 1]
        source = own_ref if step == 1 else before

        def put(f, r, value, after=after):
            put_row(after, f, r, value)

        run_sweeps(
            [
                Sweep(
                    (2 * step - 1, sh.height - 2 * step + 1),
                    (2 * step, sh.height - 2 * step),
                    functools.partial(row, source),
                    functools.partial(coef, own_ref.at[COEF]),
                    put,
                )
            ]
        )


def edges_kernel(sh, own_ref, ra_ref, rb_ref, start_ref, coef_ref, hist_ref):
    even = even_lon()
    lane = lane_ids()
    low = lane < HALF
    half_lane = lane & (HALF - 1)
    west_halo = half_lane < HALO
    east_own = (half_lane >= EAST0) & (half_lane < EAST0 + 2 * HALO)
    east_halo = (half_lane >= EAST0 + 2 * HALO) & (half_lane < EAST0 + 3 * HALO)
    sign = north_sign()

    def from_east(v):
        return jnp.where(even, ra_ref[v], rb_ref[v])

    def from_west(v):
        return jnp.where(even, rb_ref[v], ra_ref[v])

    def edge_row(f, k):
        own = own_columns(row(own_ref, f, k - HALO), row(own_ref, f, sh.ext - 1 - k - HALO))
        v, at = sh.strip(k, f)
        w, e = roll(from_west(v), -at), roll(from_east(v), EAST0 + 2 * HALO - at)
        i = sh.ext - 1 - k - sh.fold_first
        if i >= 0:
            v, h = f * PAIRS + i % PAIRS, HALF * (i // PAIRS)
            w2 = roll(from_west(v), HALF - (h + HALF - HALO))
            e2 = roll(from_east(v), HALF + EAST0 + 2 * HALO - h)
        yield
        value = merge_own(own, low, east_own)
        if i >= 0:
            w, e = jnp.where(low, w, w2), jnp.where(low, e, e2)
        value = jnp.where(west_halo, w, jnp.where(east_halo, e, value))
        if f == COEF:
            put_edge_coefs(coef_ref, k - HALO, value, sign)
        else:
            put_row(start_ref, f, k - HALO, value)

    run_staged([edge_row(f, k) for k in range(HALO, sh.mid) for f in range(FIELDS)], 4)

    rows = sh.mid - HALO
    for step in range(1, SUBCYCLES + 1):
        source = start_ref if step == 1 else hist_ref.at[step - 2]
        after = hist_ref.at[step - 1]

        def put(f, r, value, after=after):
            put_row(after, f, r, value)

        run_sweeps(
            [
                Sweep(
                    (2 * step - 1, rows),
                    (2 * step, rows),
                    functools.partial(row, source),
                    functools.partial(coef, coef_ref),
                    put,
                    mirror=rows,
                )
            ]
        )


def own_columns(a, b):
    east = EAST0 - (LANES - 2 * HALO)
    return roll(a, HALO), roll(a, east), roll(b, HALF + HALO), roll(b, HALF + east)


def merge_own(parts, low, east_own):
    aw, ae, bw, be = parts
    return jnp.where(east_own, jnp.where(low, ae, be), jnp.where(low, aw, bw))


def put_edge_coefs(ref, k, value, sign):
    at = SUBLANES * k
    thick = value[0:1]
    ref[at : at + 2, :] = value[0:2]
    ref[at + 2 : at + 3, :] = value[2:3] * sign[0:1]
    ref[at + 3 : at + 4, :] = value[3:4]
    ref[at + WET : at + WET + 1, :] = jnp.where(thick > 0, 1.0, 0.0).astype(F32)
    ref[at + NORTH_THICK : at + NORTH_THICK + 1, :] = thick * sign[0:1]


class Wedges:
    def __init__(self, sh, own_ref, hist_ref, start_ref, ecoef_ref, ehist_ref, buffers):
        self.sh, self.own, self.hist = sh, own_ref, hist_ref
        self.start, self.ecoef, self.ehist = start_ref, ecoef_ref, ehist_ref
        self.main, self.main_c, self.edge, self.edge_c = buffers
        lane = lane_ids()
        self.low = lane < HALF
        self.half_lane = half = lane & (HALF - 1)
        self.east_own = (half >= EAST0) & (half < EAST0 + 2 * HALO)
        self.halo = (half < HALO) | ((half >= EAST0 + 2 * HALO) & (half < EAST0 + 3 * HALO))
        self.sign = north_sign()

    SHAPES = (
        (STATE, 4 * HALO * SUBLANES, LANES),
        (4 * HALO * SUBLANES, LANES),
        (FIELDS, 2 * HALO * SUBLANES, LANES),
        (HALO * SUBLANES, LANES),
    )

    def at(self, r):
        span = 2 * HALO
        return r if r < span else r - (self.sh.ext - span) + span

    def main_row(self, f, r):
        if f == COEF:
            at = SUBLANES * self.at(r)
            return self.main_c[at : at + SUBLANES, :]
        return row(self.main, f, self.at(r))

    def put_main(self, f, r, value):
        if f < STATE:
            put_row(self.main, f, self.at(r), value)
            return
        at = SUBLANES * self.at(r)
        self.main_c[at : at + SUBLANES, :] = value
        self.main_c[at + WET : at + WET + 1, :] = jnp.where(value[0:1] > 0, 1.0, 0.0).astype(F32)

    def put_halo(self, f, r, value):
        north = r >= self.sh.mid
        k, base = (self.sh.ext - 1 - r, HALF) if north else (r, 0)
        self.edge[f, SUBLANES * k : SUBLANES * (k + 1), base : base + HALF] = value[
            :, base : base + HALF
        ]

    def take_band(self, ref, corners, north):
        base = HALF if north else 0

        def band_row(f, i):
            r = self.sh.ext - HALO + i if north else i
            if f < STATE:
                value = ref[f * HALO + i]
            else:
                value = ref[STATE * HALO + i % PAIRS]
                value = value if i < PAIRS else roll(value, SUBLANES // 2, 0)
            v, at = self.sh.corner(i, f)
            v = corners[v - self.sh.main]
            w, e = roll(v, base - at), roll(v, base + EAST0 + HALO - at)
            yield
            self.put_main(f, r, value)
            self.put_halo(f, r, jnp.where(self.half_lane < HALO, w, e))

        run_staged([band_row(f, i) for f in range(FIELDS) for i in range(HALO)], 10)

    def no_band(self, north):
        zero = jnp.zeros((SUBLANES, LANES), F32)
        for f in range(FIELDS):
            for i in range(HALO):
                r = self.sh.ext - HALO + i if north else i
                self.put_main(f, r, zero)
                self.put_halo(f, r, zero)

    def edge_rows(self, north_only=False):
        def edge_row(f, k):
            b = self.main_row(f, self.sh.ext - 1 - k)
            parts = own_columns(b if north_only else self.main_row(f, k), b)
            yield
            value = jnp.where(
                self.halo, row(self.edge, f, k), merge_own(parts, self.low, self.east_own)
            )
            if f == COEF:
                put_edge_coefs(self.edge_c, k, value, self.sign)
            else:
                put_row(self.edge, f, k, value)

        run_staged([edge_row(f, k) for k in range(HALO) for f in range(FIELDS)], 8)

    def steps(self, sides):
        ext = self.sh.ext

        def put_edge(f, k, value):
            put_row(self.edge, f, k, value)

        def edge_coef(k, c):
            return coef(self.edge_c, k, c) if k < HALO else coef(self.ecoef, k - HALO, c)

        def main_coef(r, c):
            if HALO <= r < ext - HALO:
                return coef(self.own.at[COEF], r - HALO, c)
            return coef(self.main_c, self.at(r), c)

        for step in range(1, SUBCYCLES + 1):
            source = self.own if step == 1 else self.hist.at[step - 2]
            e_source = self.start if step == 1 else self.ehist.at[step - 2]
            after, e_after = self.hist.at[step - 1], self.ehist.at[step - 1]
            first, ready = 2 * step - 2, 2 * step + HALO - 2

            def old_main(f, r, source=source, ready=ready):
                if ready <= r < ext - ready:
                    return row(source, f, r - HALO)
                return self.main_row(f, r)

            def old_edge(f, k, e_source=e_source, ready=ready):
                return row(e_source, f, k - HALO) if k >= ready else row(self.edge, f, k)

            def known_main(r, after=after):
                return row(after, 0, r - HALO)

            def known_edge(k, e_after=e_after):
                return row(e_after, 0, k - HALO)

            elev, vel = (first + 1, ready + 1), (first + 2, ready + 2)
            sweeps = [
                Sweep(elev, vel, old_edge, edge_coef, put_edge, known_edge, mirror=self.sh.mid)
            ]
            if "south" in sides:
                sweeps.append(Sweep(elev, vel, old_main, main_coef, self.put_main, known_main))
            if "north" in sides:
                elev, vel = [(ext - rows[1], ext - rows[0]) for rows in (elev, vel)]
                sweeps.append(Sweep(elev, vel, old_main, main_coef, self.put_main, known_main))
            run_sweeps(sweeps)

    def output(self, first, last, put):
        ext, mid, ready = self.sh.ext, self.sh.mid, 2 * HALO
        final, e_final = self.hist.at[SUBCYCLES - 1], self.ehist.at[SUBCYCLES - 1]
        lane = lane_ids()

        def output_row(f, r):
            k, h = (r, 0) if r < mid else (ext - 1 - r, HALF)
            v = row(self.edge, f, k) if k < ready else row(e_final, f, k - HALO)
            w, e = roll(v, -(h + HALO)), roll(v, LANES - HALO - (h + EAST0 + HALO))
            yield
            inner = ready <= r < ext - ready
            v = row(final, f, r - HALO) if inner else self.main_row(f, r)
            v = jnp.where(lane < HALO, w, jnp.where(lane >= LANES - HALO, e, v))
            put(f, r - HALO, v)

        run_staged([output_row(f, r) for f in range(STATE) for r in range(first, last)], 10)


def wedge_kernel(sh, sizes, n_lat, *refs):
    lat_size, _ = sizes
    bands, refs = [(refs[n], refs[n_lat + n]) for n in range(n_lat)], refs[2 * n_lat :]
    state, (out_ref, order_out), kept, buffers = refs[:5], refs[5:7], refs[7:10], refs[10:]
    wedges = Wedges(sh, *state, buffers)
    order_out[...] = jnp.zeros((SUBLANES, LANES), F32)
    for source, target in zip(state[2:], kept):
        target[...] = source[...]

    def take(band, north):
        wedges.take_band(*band, north)

    lat = lax.axis_index("lat")
    lat_even = lax.rem(lat, 2) == 0
    lat_odd = jnp.logical_not(lat_even)
    at_top = lat == lat_size - 1

    @pl.when(at_top)
    def _():
        wedges.no_band(True)

    @pl.when(lat == 0)
    def _():
        wedges.no_band(False)

    @pl.when(lat_even)
    def _():
        take(bands[0], True)

    @pl.when(lat_odd)
    def _():
        take(bands[0], False)

    if n_lat == 2:

        @pl.when(lat_odd & jnp.logical_not(at_top))
        def _():
            take(bands[1], True)

        @pl.when(lat_even & (lat > 0))
        def _():
            take(bands[1], False)

    wedges.edge_rows()
    wedges.steps(("south", "north"))

    def put(f, r, value):
        out_ref[f, pl.ds(r, SUBLANES, stride=sh.height), :] = value

    wedges.output(HALO, sh.ext - HALO, put)


def north_kernel(sh, sizes, fold_ref, order_ref, *buffers):
    @pl.when(lax.axis_index("lat") == sizes[0] - 1)
    def _():
        wedges = Wedges(sh, None, None, None, None, None, buffers)
        wedges.no_band(False)
        wedges.take_band(fold_ref, fold_ref.at[sh.main :], True)
        wedges.edge_rows(north_only=True)


def last_kernel(sh, sizes, *refs):
    lat_size, _ = sizes
    done_ref, state, begin = refs[0], refs[1:6], refs[6:10]
    out_hbm, late_ref, sems, main, edge = refs[10:]
    height, ext = sh.height, sh.ext
    split = (height - HALO) // SUBLANES * SUBLANES
    at_top = lax.axis_index("lat") == lat_size - 1
    lines = [
        [pl.ds(d * height + start, size) for d in range(SUBLANES)]
        for start, size in ((0, split), (split, height - split))
    ]

    def copies(source, part):
        return [
            pltpu.make_async_copy(
                source.at[f, line], out_hbm.at[f, line], sems.at[part, f, d]
            )
            for f in range(STATE)
            for d, line in enumerate(lines[part])
        ]

    early = copies(done_ref, 0)
    for copy in early:
        copy.start()

    @pl.when(jnp.logical_not(at_top))
    def _():
        rest = copies(done_ref, 1)
        for copy in rest:
            copy.start()
        for copy in rest:
            copy.wait()

    @pl.when(at_top)
    def _():
        wedges = Wedges(sh, *state, (main, begin[1], edge, begin[3]))
        for f in range(STATE):
            for k in range(HALO):
                put_row(edge, f, k, row(begin[2], f, k))
                at = wedges.at(ext - 1 - k)
                put_row(main, f, at, row(begin[0], f, at))
        wedges.steps(("north",))

        def put(f, r, value):
            late_ref[f, pl.ds(r, SUBLANES, stride=height), :] = value

        for f in range(STATE):
            for r in range(split, height - HALO):
                put(f, r, done_ref[f, pl.ds(r, SUBLANES, stride=height), :])
        wedges.output(ext - 2 * HALO, ext - HALO, put)
        rest = copies(late_ref, 1)
        for copy in rest:
            copy.start()
        for copy in rest:
            copy.wait()

    for copy in early:
        copy.wait()


def pair_swaps(size, wrap):
    first = [(i, i ^ 1) for i in range(size)]
    second = []
    for i in range(size):
        j = i + 1 if i % 2 else i - 1
        if wrap or 0 <= j < size:
            second.append((i, j % size))
    return first, second


def vmem(n):
    return [pl.BlockSpec(memory_space=pltpu.VMEM)] * n


def in_hbm(x):
    return pltpu.with_memory_space_constraint(x, pltpu.HBM)


def smem():
    return pl.BlockSpec(memory_space=pltpu.SMEM)


def on_device(mesh_sizes, perturb, background, land_mask, levels, fold_partner):
    lat_size, lon_size = mesh_sizes
    height = perturb.shape[2]
    sh = Shapes(height)
    sizes = (lat_size, lon_size)
    flat = perturb.reshape(STATE, SUBLANES * height, LANES)
    tile = (SUBLANES, LANES)

    def shape(n):
        return pltpu.VMEM((n,) + tile, F32)

    params = pltpu.CompilerParams(vmem_limit_bytes=16 * 1024 * 1024)
    rows = SUBLANES * height
    n_lat = 1 if lat_size == 2 else 2
    side_a, side_b, own, place, branch, *lat_rows = pl.pallas_call(
        functools.partial(sides_kernel, sh, sizes),
        out_shape=(
            shape(sh.side),
            shape(sh.side),
            pltpu.VMEM((FIELDS, rows, LANES), F32),
            pltpu.VMEM(tile, jnp.int32),
            jax.ShapeDtypeStruct((1,), jnp.int32),
        )
        + (shape(sh.main),) * n_lat,
        in_specs=[pl.BlockSpec(memory_space=pltpu.HBM)] * 5,
        out_specs=tuple(vmem(4)) + (smem(),) + tuple(vmem(n_lat)),
        scratch_shapes=[
            pltpu.VMEM(flat.shape, F32),
            pltpu.VMEM(background.shape, F32),
            pltpu.VMEM(land_mask.shape, jnp.int32),
            pltpu.VMEM(levels.shape, jnp.int32),
            pltpu.SMEM(fold_partner.shape, jnp.int32),
            pltpu.SemaphoreType.DMA((4 + STATE,)),
        ],
        compiler_params=params,
        name="sides",
    )(*[in_hbm(v) for v in (flat, background, land_mask, levels, fold_partner)])

    got_a, got_b = [
        lax.ppermute(x, "lon", swap)
        for x, swap in zip((side_a, side_b), pair_swaps(lon_size, True))
    ]
    lat_swaps = pair_swaps(lat_size, False)[:n_lat]
    got_lat = [lax.ppermute(x, "lat", swap) for x, swap in zip(lat_rows, lat_swaps)]
    hist = pl.pallas_call(
        functools.partial(middle_kernel, sh),
        out_shape=pltpu.VMEM((SUBCYCLES, STATE, rows, LANES), F32),
        in_specs=vmem(1),
        out_specs=vmem(1)[0],
        compiler_params=params,
        name="middle",
    )(own)
    fold_band, *lat_corners = pl.pallas_call(
        functools.partial(bands_kernel, sh, sizes),
        out_shape=(shape(sh.band),) + (shape(sh.corners),) * n_lat,
        in_specs=vmem(4),
        out_specs=tuple(vmem(1 + n_lat)),
        compiler_params=params,
        name="bands",
    )(own, got_a, got_b, place)

    edge_rows = SUBLANES * (sh.mid - HALO)
    edge_shapes = (
        pltpu.VMEM((STATE, edge_rows, LANES), F32),
        pltpu.VMEM((edge_rows, LANES), F32),
        pltpu.VMEM((SUBCYCLES, STATE, edge_rows, LANES), F32),
    )
    step_edges = jax.jit(
        pl.pallas_call(
            functools.partial(edges_kernel, sh),
            out_shape=edge_shapes,
            in_specs=vmem(3),
            out_specs=tuple(vmem(3)),
            compiler_params=params,
            name="edges",
        )
    )
    step_wedges = jax.jit(
        pl.pallas_call(
            functools.partial(wedge_kernel, sh, sizes, n_lat),
            out_shape=(pltpu.VMEM(flat.shape, F32), pltpu.VMEM(tile, F32)) + edge_shapes,
            in_specs=vmem(2 * n_lat + 5),
            out_specs=tuple(vmem(5)),
            scratch_shapes=[pltpu.VMEM(x, F32) for x in Wedges.SHAPES],
            compiler_params=params,
            name="wedges",
        )
    )
    take_north = jax.jit(
        pl.pallas_call(
            functools.partial(north_kernel, sh, sizes),
            out_shape=tuple(pltpu.VMEM(x, F32) for x in Wedges.SHAPES),
            in_specs=vmem(2),
            out_specs=tuple(vmem(4)),
            compiler_params=params,
            name="north",
        )
    )
    top = lat_size - 1

    def rest(q, fold_band, lat_corners, got_lat, own, hist, got_a, got_b):
        across = []
        for m in range(lon_size):
            j = (q - m) % lon_size
            across.append((m * lat_size + top, j * lat_size + top))
        got_fold = lax.ppermute(fold_band, ("lon", "lat"), across)
        got_corners = [lax.ppermute(x, "lat", swap) for x, swap in zip(lat_corners, lat_swaps)]
        edges = step_edges(own, got_a, got_b)
        done, order, *kept = step_wedges(*got_lat, *got_corners, own, hist, *edges)
        return kept, done, take_north(got_fold, order)

    edges, done, beyond = lax.switch(
        branch[0],
        [functools.partial(rest, q) for q in range(lon_size)],
        fold_band,
        lat_corners,
        got_lat,
        own,
        hist,
        got_a,
        got_b,
    )
    out = pl.pallas_call(
        functools.partial(last_kernel, sh, sizes),
        out_shape=jax.ShapeDtypeStruct(flat.shape, F32),
        in_specs=vmem(10),
        out_specs=pl.BlockSpec(memory_space=pltpu.HBM),
        scratch_shapes=[
            pltpu.VMEM(flat.shape, F32),
            pltpu.SemaphoreType.DMA((2, STATE, SUBLANES)),
            pltpu.VMEM(Wedges.SHAPES[0], F32),
            pltpu.VMEM(Wedges.SHAPES[2], F32),
        ],
        compiler_params=params,
        name="last",
    )(done, own, hist, *edges, *beyond)
    return out.reshape(perturb.shape)


def solution(mesh):
    placed = (
        P("grp", "dir", "lat", "lon"),
        P("grp", "lat", "lon"),
        P("lat", "lon"),
        P("lat", "lon"),
        P(),
    )
    sizes = (mesh.shape["lat"], mesh.shape["lon"])
    return jax.shard_map(
        functools.partial(on_device, sizes),
        mesh=mesh,
        in_specs=placed,
        out_specs=P("grp", "dir", "lat", "lon"),
        check_vma=False,
    )
```

profile of v0, /device:TPU:0, one launch (start us, length us, event | category | flops | bytes accessed | tf_op | source)
XLA Modules:
  0.0 24.9 jit_solution(14664187653411999905)
XLA Ops:
  0.0 2.1 %sides.1 = (f32[31,8,128]{2,1,0:T(8,128)S(1)}, f32[31,8,128]{2,1,0:T(8,128)S(1)}, f32[4,256,128]{2,1,0:T(8,128)S(1)}, s32[8,128]{1,0:T(8,128)S(1)}, s32[1]{0:T(128)}, /*index=5*/f32[35,8,128]{2,1,0:T(8,128)S(1)}) custom-call(f32[3,256,128]{2,1,0:T(8,128)} %bitcast.3, f32[3,32,128]{2,1,0:T(8,128)} %b_hbm.1, s32[32,128]{1,0:T(8,128)} %m_hbm.1, ...), custom_call_target="tpu_custom_call" | custom-call | tf_op jit(solution)/shard_map/sides/pallas_call | solution.py:837
  2.1 3.0 %collective-permute-start.10 = (f32[35,8,128]{2,1,0:T(8,128)S(1)}, f32[35,8,128]{2,1,0:T(8,128)S(1)}, u32[]{:S(2)}, u32[]{:S(2)}) collective-permute-start(f32[35,8,128]{2,1,0:T(8,128)S(1)} %get-tuple-element.159), channel_id=1, source_target_pairs={{0,2},{2,0},{1,3},{3,1},{4,6},{6,4},{5,7},{7,5},{8,10},{10,8},{9,1... | collective-permute-start | bytes 430088 | tf_op jit(solution)/shard_map/ppermute | solution.py:866
  5.1 1.6 %collective-permute-start.8 = (f32[31,8,128]{2,1,0:T(8,128)S(1)}, f32[31,8,128]{2,1,0:T(8,128)S(1)}, u32[]{:S(2)}, u32[]{:S(2)}) collective-permute-start(f32[31,8,128]{2,1,0:T(8,128)S(1)} %get-tuple-element.155), channel_id=1, source_target_pairs={{0,4},{4,0},{8,12},{12,8},{1,5},{5,1},{9,13},{13,9},{2,6},{6,2},{1... | collective-permute-start | bytes 380936 | tf_op jit(solution)/shard_map/ppermute | solution.py:862
  6.7 2.5 %collective-permute-start.9 = (f32[31,8,128]{2,1,0:T(8,128)S(1)}, f32[31,8,128]{2,1,0:T(8,128)S(1)}, u32[]{:S(2)}, u32[]{:S(2)}) collective-permute-start(f32[31,8,128]{2,1,0:T(8,128)S(1)} %get-tuple-element.156), channel_id=1, source_target_pairs={{0,12},{4,8},{8,4},{12,0},{1,13},{5,9},{9,5},{13,1},{2,14},{6,10},... | collective-permute-start | bytes 380936 | tf_op jit(solution)/shard_map/ppermute | solution.py:862
  9.2 0.9 %middle.1.refs_2_ = f32[5,3,256,128]{3,2,1,0:T(8,128)S(1)} custom-call(f32[4,256,128]{2,1,0:T(8,128)S(1)} %get-tuple-element.154.own_ref.refs_1_), custom_call_target="tpu_custom_call" | custom-call | tf_op jit(solution)/shard_map/middle/pallas_call | solution.py:867
  10.8 0.0 collective-permute-done.8.ra_ref
  10.8 4.0 %collective-permute-done.9.rb_ref = f32[31,8,128]{2,1,0:T(8,128)S(1)} collective-permute-done((f32[31,8,128]{2,1,0:T(8,128)S(1)}, f32[31,8,128]{2,1,0:T(8,128)S(1)}, u32[]{:S(2)}, u32[]{:S(2)}) %collective-permute-start.9) | collective-permute-done | bytes 127008 | tf_op jit(solution)/shard_map/ppermute | solution.py:862
  14.8 0.2 bands.1
  14.9 0.0 collective-permute-done.10
  14.9 8.7 %conditional.1 = (f32[3,128,128]{2,1,0:T(8,128)S(1)}, f32[128,128]{1,0:T(8,128)S(1)}, f32[5,3,128,128]{3,2,1,0:T(8,128)S(1)}, f32[3,256,128]{2,1,0:T(8,128)S(1)}...) conditional(s32[]{:T(128)} %bitcast.1, ...), branch_computations={%region_0.1_spmd, %region_1.2_spmd, %region_2.3_spmd, %region_3.4_... | conditional | bytes 802960 | solution.py:934
  15.0 0.7 %collective-permute-start.5 = (f32[42,8,128]{2,1,0:T(8,128)S(1)}, f32[42,8,128]{2,1,0:T(8,128)S(1)}, u32[]{:S(2)}, u32[]{:S(2)}) collective-permute-start(f32[42,8,128]{2,1,0:T(8,128)S(1)} %get-tuple-element.112), channel_id=1, source_target_pairs={{2,10},{6,6},{10,2},{14,14},{3,11},{7,7},{11,3},{15,15},{18,26},{2... | collective-permute-start | bytes 516104 | tf_op jit(solution)/shard_map/cond/branch_2_fun/ppermute | solution.py:928
  15.7 4.2 %collective-permute-start.4 = (f32[7,8,128]{2,1,0:T(8,128)S(1)}, f32[7,8,128]{2,1,0:T(8,128)S(1)}, u32[]{:S(2)}, u32[]{:S(2)}) collective-permute-start(f32[7,8,128]{2,1,0:T(8,128)S(1)} %get-tuple-element.100), channel_id=1, source_target_pairs={{0,2},{2,0},{1,3},{3,1},{4,6},{6,4},{5,7},{7,5},{8,10},{10,8},{9,1... | collective-permute-start | bytes 86024 | tf_op jit(solution)/shard_map/cond/branch_2_fun/ppermute | solution.py:929
  19.8 1.2 %edges.6 = (f32[3,128,128]{2,1,0:T(8,128)S(1)}, f32[128,128]{1,0:T(8,128)S(1)}, f32[5,3,128,128]{3,2,1,0:T(8,128)S(1)}) custom-call(f32[4,256,128]{2,1,0:T(8,128)S(1)} %get-tuple-element.101.own_ref.refs_2_, f32[31,8,128]{2,1,0:T(8,128)S(1)} %get-tuple-element.103.ra_ref, f32[31,8,128]{2,1,0:T(8,128)S(1)} %get-tuple-element.104.rb_ref), custom_call_target="tpu_custom_call" | custom-call | tf_op jit(solution)/shard_map/cond/branch_2_fun/jit(wrapped)/edges/pallas_call | solution.py:930
  21.0 0.7 %collective-permute-done.4.refs_1_ = f32[7,8,128]{2,1,0:T(8,128)S(1)} collective-permute-done((f32[7,8,128]{2,1,0:T(8,128)S(1)}, f32[7,8,128]{2,1,0:T(8,128)S(1)}, u32[]{:S(2)}, u32[]{:S(2)}) %collective-permute-start.4) | collective-permute-done | bytes 28704 | tf_op jit(solution)/shard_map/cond/branch_2_fun/ppermute | solution.py:929
  21.7 1.9 %wedges.6 = (f32[3,256,128]{2,1,0:T(8,128)S(1)}, f32[8,128]{1,0:T(8,128)S(1)}, f32[3,128,128]{2,1,0:T(8,128)S(1)}, f32[128,128]{1,0:T(8,128)S(1)}, f32[5,3,128,128]{3,2,1,0:T(8,128)S(1)}) custom-call(f32[35,8,128]{2,1,0:T(8,128)S(1)} %get-tuple-element.99.refs_0_, f32[7,8,128]{2,1,0:T(8,128)S(1)} %collective-permute-done.4.refs_1_, ...), custom_call_target="tpu_custom_call" | custom-call | tf_op jit(solution)/shard_map/cond/branch_2_fun/jit(wrapped)/wedges/pallas_call | solution.py:931
  23.6 0.0 collective-permute-done.5.fold_ref
  23.6 1.2 %last.1 = f32[3,256,128]{2,1,0:T(8,128)} custom-call(f32[3,256,128]{2,1,0:T(8,128)S(1)} %get-tuple-element.161.refs_0_, f32[4,256,128]{2,1,0:T(8,128)S(1)} %get-tuple-element.154.own_ref.refs_1_, f32[5,3,256,128]{3,2,1,0:T(8,128)S(1)} %middle.1.refs_2_, f32[3,128,128]{2,1,0:T(8,128)S(1)} %get-tuple-element.162.refs_3_, ...), custom_call_target="tpu_custom_call" | custom-call | tf_op jit(solution)/shard_map/last/pallas_call | solution.py:945
  (1 shorter events, 0.0 us)
Async XLA Ops:
  2.1 12.9 %collective-permute-start.10 = (f32[35,8,128]{2,1,0:T(8,128)S(1)}, f32[35,8,128]{2,1,0:T(8,128)S(1)}, u32[]{:S(2)}, u32[]{:S(2)}) collective-permute-start(f32[35,8,128]{2,1,0:T(8,128)S(1)} %get-tuple-element.159), channel_id=1, source_target_pairs={{0,2},{2,0},{1,3},{3,1},{4,6},{6,4},{5,7},{7,5},{8,10},{10,8},{9,1... | collective-permute-start | bytes 430088 | tf_op jit(solution)/shard_map/ppermute | solution.py:866
  5.1 5.7 %collective-permute-start.8 = (f32[31,8,128]{2,1,0:T(8,128)S(1)}, f32[31,8,128]{2,1,0:T(8,128)S(1)}, u32[]{:S(2)}, u32[]{:S(2)}) collective-permute-start(f32[31,8,128]{2,1,0:T(8,128)S(1)} %get-tuple-element.155), channel_id=1, source_target_pairs={{0,4},{4,0},{8,12},{12,8},{1,5},{5,1},{9,13},{13,9},{2,6},{6,2},{1... | collective-permute-start | bytes 380936 | tf_op jit(solution)/shard_map/ppermute | solution.py:862
  6.7 8.1 %collective-permute-start.9 = (f32[31,8,128]{2,1,0:T(8,128)S(1)}, f32[31,8,128]{2,1,0:T(8,128)S(1)}, u32[]{:S(2)}, u32[]{:S(2)}) collective-permute-start(f32[31,8,128]{2,1,0:T(8,128)S(1)} %get-tuple-element.156), channel_id=1, source_target_pairs={{0,12},{4,8},{8,4},{12,0},{1,13},{5,9},{9,5},{13,1},{2,14},{6,10},... | collective-permute-start | bytes 380936 | tf_op jit(solution)/shard_map/ppermute | solution.py:862
  15.0 8.6 %collective-permute-start.5 = (f32[42,8,128]{2,1,0:T(8,128)S(1)}, f32[42,8,128]{2,1,0:T(8,128)S(1)}, u32[]{:S(2)}, u32[]{:S(2)}) collective-permute-start(f32[42,8,128]{2,1,0:T(8,128)S(1)} %get-tuple-element.112), channel_id=1, source_target_pairs={{2,10},{6,6},{10,2},{14,14},{3,11},{7,7},{11,3},{15,15},{18,26},{2... | collective-permute-start | bytes 516104 | tf_op jit(solution)/shard_map/cond/branch_2_fun/ppermute | solution.py:928
  15.7 6.0 %collective-permute-start.4 = (f32[7,8,128]{2,1,0:T(8,128)S(1)}, f32[7,8,128]{2,1,0:T(8,128)S(1)}, u32[]{:S(2)}, u32[]{:S(2)}) collective-permute-start(f32[7,8,128]{2,1,0:T(8,128)S(1)} %get-tuple-element.100), channel_id=1, source_target_pairs={{0,2},{2,0},{1,3},{3,1},{4,6},{6,4},{5,7},{7,5},{8,10},{10,8},{9,1... | collective-permute-start | bytes 86024 | tf_op jit(solution)/shard_map/cond/branch_2_fun/ppermute | solution.py:929
where the time goes:
time: 25 us; the launch traced here: 24.9 us
  starting transfers between devices  11.9 us (48%)
  Pallas kernels  7.55 us (30%)
  waiting for transfers between devices  4.67 us (19%)
  between operations  0.7 us (3%)
    ppermute x1, starting transfers between devices, rest(): lax.ppermute(x, 'lat', swap)  4.16 us
    ppermute x2, starting transfers between devices, on_device(): lax.ppermute(x, 'lon', swap)  4.05 us
    ppermute x2, waiting for transfers between devices, on_device(): lax.ppermute(x, 'lon', swap)  4 us
    ppermute x1, starting transfers between devices, on_device(): lax.ppermute(x, 'lat', swap)  3.01 us
    pallas_call x1, Pallas kernels, on_device(): pl.pallas_call(functools.partial(sides_kernel, sh, sizes), out_shape=(sha...  2.08 us
    pallas_call x1, Pallas kernels, rest(): done, order, *kept = step_wedges(*got_lat, *got_corners, own, hist, *edges)  1.92 us
    pallas_call x1, Pallas kernels, on_device(): pl.pallas_call(functools.partial(last_kernel, sh, sizes), out_shape=jax.S...  1.25 us
    pallas_call x1, Pallas kernels, rest(): edges = step_edges(own, got_a, got_b)  1.19 us
  transfers between devices with their start and end apart: 5, of which 2 were waited for; matrix products, arithmetic and copies ran while one was open for 0% of the time, Pallas kernels for 17%

commit v1 on v0

--- a/solution.py
+++ b/solution.py
@@ -36,17 +36,27 @@
         self.ext = height + 2 * HALO
         self.mid = self.ext // 2
         self.fold_first = height
-        self.blocks = FIELDS * PAIRS
-        self.strip_rows = height // 2
-        self.strips = ceil_div(self.strip_rows * FIELDS, STRIP_SLOTS)
-        self.side = self.blocks + self.strips
+        self.blocks = STATE * PAIRS + ceil_div(PAIRS, 2)
+        self.strip_rows = self.mid - HALO
+        self.strip_pairs = self.strip_rows // 2
+        slots = self.strip_rows * STATE + self.strip_pairs
+        self.side = self.blocks + ceil_div(slots, STRIP_SLOTS)
         self.main = STATE * HALO + PAIRS
         self.corners = ceil_div(FIELDS * HALO, CORNER_SLOTS)
         self.band = self.main + self.corners
 
+    def block(self, i, f):
+        upper = i // PAIRS
+        if f < STATE:
+            return f * PAIRS + i % PAIRS, upper, False
+        return STATE * PAIRS + i % PAIRS // 2, i % PAIRS % 2, upper == 1
+
     def strip(self, k, f):
-        slot = (k - HALO) * FIELDS + f
-        return self.blocks + slot // STRIP_SLOTS, HALO * (slot % STRIP_SLOTS)
+        slot, upper = (k - HALO) * STATE + f, False
+        if f == COEF:
+            upper = k - HALO >= self.strip_pairs
+            slot = self.strip_rows * STATE + (k - HALO) % self.strip_pairs
+        return self.blocks + slot // STRIP_SLOTS, HALO * (slot % STRIP_SLOTS), upper
 
     def corner(self, i, f):
         slot = f * HALO + i
@@ -98,6 +108,10 @@
 
 def put_row(ref, f, r, value):
     ref[f, SUBLANES * r : SUBLANES * (r + 1), :] = value
+
+
+def flat_rows(ref):
+    return ref.reshape(ref.shape[0], ref.shape[1] * ref.shape[2], ref.shape[3])
 
 
 def coef(ref, r, c):
@@ -120,6 +134,34 @@
 
 def pair_coefs(a, b):
     return jnp.where(sublane_ids() < SUBLANES // 2, a, roll(b, SUBLANES // 2, 0))
+
+
+def lat_rows(sh, own_ref, outs):
+    own = functools.partial(row, own_ref)
+
+    def raw_rows(out, first):
+        for f in range(STATE):
+            for i in range(HALO):
+                out[f * HALO + i] = own(f, first + i)
+        for i in range(PAIRS):
+            out[STATE * HALO + i] = pair_coefs(
+                own(COEF, first + i), own(COEF, first + i + PAIRS)
+            )
+
+    top = sh.height - HALO
+    lat_even = lax.rem(lax.axis_index("lat"), 2) == 0
+
+    @pl.when(lat_even)
+    def _():
+        raw_rows(outs[0], top)
+        if len(outs) > 1:
+            raw_rows(outs[1], 0)
+
+    @pl.when(jnp.logical_not(lat_even))
+    def _():
+        raw_rows(outs[0], 0)
+        if len(outs) > 1:
+            raw_rows(outs[1], top)
 
 
 def sides_kernel(sh, sizes, x_hbm, b_hbm, m_hbm, l_hbm, p_hbm, *rest):
@@ -166,41 +208,58 @@
             put_row(own_ref, f, r, x_ref[f, pl.ds(r, SUBLANES, stride=height), :])
 
     even = even_lon()
-    lane = lane_ids()
+    lane, sub = lane_ids(), sublane_ids()
     low = lane < HALF
     own = functools.partial(row, own_ref)
     top = height - HALO
 
-    def block(f, i):
-        a, b = own(f, top + i), own(f, top + i + PAIRS)
+    def rows_of(f, r):
+        return pair_coefs(own(f, r), own(f, r + PAIRS)) if f == COEF else own(f, r)
+
+    def strip_rows_of(f, r, other):
+        return pair_coefs(own(f, r), own(f, other)) if f == COEF else own(f, r)
+
+    def block(v, a, b):
         a_up, b_up = roll(a, HALF), roll(b, HALF)
         yield
         east = jnp.where(low, a_up, b)
         west = jnp.where(low, a, b_up)
-        v = f * PAIRS + i
         a_out[v] = jnp.where(even, east, west)
         b_out[v] = jnp.where(even, west, east)
+
+    def blocks():
+        for f in range(STATE):
+            for i in range(PAIRS):
+                yield block(f * PAIRS + i, own(f, top + i), own(f, top + i + PAIRS))
+        for i in range(0, PAIRS, 2):
+            v, _, _ = sh.block(i, COEF)
+            yield block(v, rows_of(COEF, top + i), rows_of(COEF, top + min(i + 1, PAIRS - 1)))
 
     slots = {}
     for k in range(HALO, sh.mid):
         for f in range(FIELDS):
-            v, at = sh.strip(k, f)
-            slots.setdefault(v, []).append((k, f, at))
+            v, at, upper = sh.strip(k, f)
+            if not upper:
+                slots.setdefault(v, []).append((k, f, at))
 
     def strips(v):
         parts = []
         for k, f, at in slots[v]:
-            a, b = own(f, k - HALO), own(f, sh.ext - 1 - k - HALO)
-            beyond = HALF if sh.ext - 1 - k >= sh.fold_first else 0
-            parts.append(
-                (
-                    at,
-                    roll(a, at - (LANES - HALO)),
-                    roll(b, HALF + at - (LANES - HALO) + beyond),
-                    roll(a, at),
-                    roll(b, HALF + at - beyond),
-                )
-            )
+            ahead = sh.strip_pairs
+            r = sh.ext - 1 - k - HALO
+            a, b = strip_rows_of(f, k - HALO, k - HALO + ahead), strip_rows_of(f, r, r - ahead)
+            end = at - (LANES - HALO)
+            a_east, a_west = roll(a, end), roll(a, at)
+            near = sh.ext - 1 - k < sh.fold_first
+            near_other = sh.ext - 1 - k - ahead < sh.fold_first
+            b_east, b_west = roll(b, HALF + end), roll(b, HALF + at)
+            if not near:
+                b_east, b_west = roll(b, end), roll(b, at)
+                if f == COEF and near_other:
+                    lower_half = sub < SUBLANES // 2
+                    b_east = jnp.where(lower_half, b_east, roll(b, HALF + end))
+                    b_west = jnp.where(lower_half, b_west, roll(b, HALF + at))
+            parts.append((at, a_east, b_east, a_west, b_west))
         yield
         east = west = jnp.zeros((SUBLANES, LANES), F32)
         for at, ea, eb, wa, wb in parts:
@@ -211,31 +270,9 @@
         a_out[v] = jnp.where(even, east, west)
         b_out[v] = jnp.where(even, west, east)
 
-    run_staged([block(f, i) for f in range(FIELDS) for i in range(PAIRS)], 10)
+    run_staged(blocks(), 10)
     run_staged([strips(v) for v in sorted(slots)], 2)
-
-    def raw_rows(out, first):
-        for f in range(STATE):
-            for i in range(HALO):
-                out[f * HALO + i] = own(f, first + i)
-        for i in range(PAIRS):
-            out[STATE * HALO + i] = pair_coefs(
-                own(COEF, first + i), own(COEF, first + i + PAIRS)
-            )
-
-    lat_even = lax.rem(lax.axis_index("lat"), 2) == 0
-
-    @pl.when(lat_even)
-    def _():
-        raw_rows(lat_outs[0], top)
-        if len(lat_outs) > 1:
-            raw_rows(lat_outs[1], 0)
-
-    @pl.when(jnp.logical_not(lat_even))
-    def _():
-        raw_rows(lat_outs[0], 0)
-        if len(lat_outs) > 1:
-            raw_rows(lat_outs[1], top)
+    lat_rows(sh, own_ref, lat_outs)
 
 
 def bands_kernel(sh, sizes, own_ref, ra_ref, rb_ref, place_ref, fold_out, *lat_outs):
@@ -246,25 +283,25 @@
     own = functools.partial(row, own_ref)
     top = sh.height - HALO
 
-    def from_east(v):
-        return jnp.where(even, ra_ref[v], rb_ref[v])
-
-    def from_west(v):
-        return jnp.where(even, rb_ref[v], ra_ref[v])
+    def got(v, upper):
+        a, b = ra_ref[v], rb_ref[v]
+        w, e = jnp.where(even, b, a), jnp.where(even, a, b)
+        if upper:
+            w, e = roll(w, SUBLANES // 2, 0), roll(e, SUBLANES // 2, 0)
+        return w, e
 
     def corners(out, is_top):
         def register(v, items):
             parts = []
             for i, f, at in items:
                 if is_top:
-                    src, h = f * PAIRS + i % PAIRS, HALF * (i // PAIRS)
-                    w_at, e_at = h + HALF - HALO, h
+                    src, h, upper = sh.block(i, f)
+                    w_at, e_at = HALF * h + HALF - HALO, HALF * h
                 else:
-                    src, w_at = sh.strip(HALO + i, f)
+                    src, w_at, upper = sh.strip(HALO + i, f)
                     e_at = w_at
-                parts.append(
-                    (at, roll(from_west(src), at - w_at), roll(from_east(src), at + HALO - e_at))
-                )
+                w, e = got(src, upper)
+                parts.append((at, roll(w, at - w_at), roll(e, at + HALO - e_at)))
             yield
             total = jnp.zeros((SUBLANES, LANES), F32)
             for at, w, e in parts:
@@ -305,15 +342,15 @@
         coef_signs = jnp.where((sub == 1) | (sub == 2), -1.0, 1.0).astype(F32)
 
         def reversed_row(f, i):
-            v, h = f * PAIRS + i % PAIRS, i // PAIRS
-            w, e = from_west(v), from_east(v)
+            v, h, upper = sh.block(i, f)
+            w, e = got(v, upper)
             if h == 0:
                 w = roll(w, HALF)
             else:
                 e = roll(e, HALF)
-            v, at = sh.strip(sh.ext - 1 - sh.fold_first - i, f)
-            far_w = roll(from_west(v), HALF - HALO - HALF - at)
-            far_e = roll(from_east(v), -at)
+            v, at, upper = sh.strip(sh.ext - 1 - sh.fold_first - i, f)
+            far_w, far_e = got(v, upper)
+            far_w, far_e = roll(far_w, -HALO - at), roll(far_e, -at)
             yield
             both = jnp.where(low, e, w)
             mine = own(f, top + i)
@@ -459,21 +496,24 @@
     east_halo = (half_lane >= EAST0 + 2 * HALO) & (half_lane < EAST0 + 3 * HALO)
     sign = north_sign()
 
-    def from_east(v):
-        return jnp.where(even, ra_ref[v], rb_ref[v])
-
-    def from_west(v):
-        return jnp.where(even, rb_ref[v], ra_ref[v])
+    def got(v, upper):
+        a, b = ra_ref[v], rb_ref[v]
+        w, e = jnp.where(even, b, a), jnp.where(even, a, b)
+        if upper:
+            w, e = roll(w, SUBLANES // 2, 0), roll(e, SUBLANES // 2, 0)
+        return w, e
 
     def edge_row(f, k):
         own = own_columns(row(own_ref, f, k - HALO), row(own_ref, f, sh.ext - 1 - k - HALO))
-        v, at = sh.strip(k, f)
-        w, e = roll(from_west(v), -at), roll(from_east(v), EAST0 + 2 * HALO - at)
+        v, at, upper = sh.strip(k, f)
+        w, e = got(v, upper)
+        w, e = roll(w, -at), roll(e, EAST0 + 2 * HALO - at)
         i = sh.ext - 1 - k - sh.fold_first
         if i >= 0:
-            v, h = f * PAIRS + i % PAIRS, HALF * (i // PAIRS)
-            w2 = roll(from_west(v), HALF - (h + HALF - HALO))
-            e2 = roll(from_east(v), HALF + EAST0 + 2 * HALO - h)
+            v, h, upper = sh.block(i, f)
+            w2, e2 = got(v, upper)
+            w2 = roll(w2, HALF - (HALF * h + HALF - HALO))
+            e2 = roll(e2, HALF + EAST0 + 2 * HALO - HALF * h)
         yield
         value = merge_own(own, low, east_own)
         if i >= 0:
@@ -572,9 +612,7 @@
             :, base : base + HALF
         ]
 
-    def take_band(self, ref, corners, north):
-        base = HALF if north else 0
-
+    def take_band(self, ref, halos, north):
         def band_row(f, i):
             r = self.sh.ext - HALO + i if north else i
             if f < STATE:
@@ -582,9 +620,7 @@
             else:
                 value = ref[STATE * HALO + i % PAIRS]
                 value = value if i < PAIRS else roll(value, SUBLANES // 2, 0)
-            v, at = self.sh.corner(i, f)
-            v = corners[v - self.sh.main]
-            w, e = roll(v, base - at), roll(v, base + EAST0 + HALO - at)
+            w, e = halos(f, i, HALF if north else 0)
             yield
             self.put_main(f, r, value)
             self.put_halo(f, r, jnp.where(self.half_lane < HALO, w, e))
@@ -687,7 +723,14 @@
         target[...] = source[...]
 
     def take(band, north):
-        wedges.take_band(*band, north)
+        ref, corners = band
+
+        def halos(f, i, base):
+            v, at = sh.corner(i, f)
+            v = corners[v - sh.main]
+            return roll(v, base - at), roll(v, base + EAST0 + HALO - at)
+
+        wedges.take_band(ref, halos, north)
 
     lat = lax.axis_index("lat")
     lat_even = lax.rem(lat, 2) == 0
@@ -723,8 +766,10 @@
     wedges.edge_rows()
     wedges.steps(("south", "north"))
 
+    out_flat = flat_rows(out_ref)
+
     def put(f, r, value):
-        out_ref[f, pl.ds(r, SUBLANES, stride=sh.height), :] = value
+        out_flat[f, pl.ds(r, SUBLANES, stride=sh.height), :] = value
 
     wedges.output(HALO, sh.ext - HALO, put)
 
@@ -734,7 +779,12 @@
     def _():
         wedges = Wedges(sh, None, None, None, None, None, buffers)
         wedges.no_band(False)
-        wedges.take_band(fold_ref, fold_ref.at[sh.main :], True)
+
+        def halos(f, i, base):
+            v, at = sh.corner(i, f)
+            return roll(fold_ref[v], base - at), roll(fold_ref[v], base + EAST0 + HALO - at)
+
+        wedges.take_band(fold_ref, halos, True)
         wedges.edge_rows(north_only=True)
 
 
@@ -745,18 +795,14 @@
     height, ext = sh.height, sh.ext
     split = (height - HALO) // SUBLANES * SUBLANES
     at_top = lax.axis_index("lat") == lat_size - 1
-    lines = [
-        [pl.ds(d * height + start, size) for d in range(SUBLANES)]
-        for start, size in ((0, split), (split, height - split))
-    ]
+    lines = (pl.ds(0, split), pl.ds(split, height - split))
 
     def copies(source, part):
         return [
             pltpu.make_async_copy(
-                source.at[f, line], out_hbm.at[f, line], sems.at[part, f, d]
+                source.at[f, :, lines[part]], out_hbm.at[f, :, lines[part]], sems.at[part, f]
             )
             for f in range(STATE)
-            for d, line in enumerate(lines[part])
         ]
 
     early = copies(done_ref, 0)
@@ -781,12 +827,14 @@
                 put_row(main, f, at, row(begin[0], f, at))
         wedges.steps(("north",))
 
+        late_flat, done_flat = flat_rows(late_ref), flat_rows(done_ref)
+
         def put(f, r, value):
-            late_ref[f, pl.ds(r, SUBLANES, stride=height), :] = value
+            late_flat[f, pl.ds(r, SUBLANES, stride=height), :] = value
 
         for f in range(STATE):
             for r in range(split, height - HALO):
-                put(f, r, done_ref[f, pl.ds(r, SUBLANES, stride=height), :])
+                put(f, r, done_flat[f, pl.ds(r, SUBLANES, stride=height), :])
         wedges.output(ext - 2 * HALO, ext - HALO, put)
         rest = copies(late_ref, 1)
         for copy in rest:
@@ -834,7 +882,7 @@
     params = pltpu.CompilerParams(vmem_limit_bytes=16 * 1024 * 1024)
     rows = SUBLANES * height
     n_lat = 1 if lat_size == 2 else 2
-    side_a, side_b, own, place, branch, *lat_rows = pl.pallas_call(
+    side_a, side_b, own, place, branch, *lat_out = pl.pallas_call(
         functools.partial(sides_kernel, sh, sizes),
         out_shape=(
             shape(sh.side),
@@ -858,12 +906,9 @@
         name="sides",
     )(*[in_hbm(v) for v in (flat, background, land_mask, levels, fold_partner)])
 
-    got_a, got_b = [
-        lax.ppermute(x, "lon", swap)
-        for x, swap in zip((side_a, side_b), pair_swaps(lon_size, True))
-    ]
-    lat_swaps = pair_swaps(lat_size, False)[:n_lat]
-    got_lat = [lax.ppermute(x, "lat", swap) for x, swap in zip(lat_rows, lat_swaps)]
+    lon_swaps = pair_swaps(lon_size, True)
+    got_a, got_b = [lax.ppermute(x, "lon", swap) for x, swap in zip((side_a, side_b), lon_swaps)]
+
     hist = pl.pallas_call(
         functools.partial(middle_kernel, sh),
         out_shape=pltpu.VMEM((SUBCYCLES, STATE, rows, LANES), F32),
@@ -872,6 +917,8 @@
         compiler_params=params,
         name="middle",
     )(own)
+    lat_swaps = pair_swaps(lat_size, False)[:n_lat]
+    got_lat = [lax.ppermute(x, "lat", swap) for x, swap in zip(lat_out, lat_swaps)]
     fold_band, *lat_corners = pl.pallas_call(
         functools.partial(bands_kernel, sh, sizes),
         out_shape=(shape(sh.band),) + (shape(sh.corners),) * n_lat,
@@ -900,7 +947,7 @@
     step_wedges = jax.jit(
         pl.pallas_call(
             functools.partial(wedge_kernel, sh, sizes, n_lat),
-            out_shape=(pltpu.VMEM(flat.shape, F32), pltpu.VMEM(tile, F32)) + edge_shapes,
+            out_shape=(pltpu.VMEM(perturb.shape, F32), pltpu.VMEM(tile, F32)) + edge_shapes,
             in_specs=vmem(2 * n_lat + 5),
             out_specs=tuple(vmem(5)),
             scratch_shapes=[pltpu.VMEM(x, F32) for x in Wedges.SHAPES],
@@ -942,21 +989,20 @@
         got_a,
         got_b,
     )
-    out = pl.pallas_call(
+    return pl.pallas_call(
         functools.partial(last_kernel, sh, sizes),
-        out_shape=jax.ShapeDtypeStruct(flat.shape, F32),
+        out_shape=jax.ShapeDtypeStruct(perturb.shape, F32),
         in_specs=vmem(10),
         out_specs=pl.BlockSpec(memory_space=pltpu.HBM),
         scratch_shapes=[
-            pltpu.VMEM(flat.shape, F32),
-            pltpu.SemaphoreType.DMA((2, STATE, SUBLANES)),
+            pltpu.VMEM(perturb.shape, F32),
+            pltpu.SemaphoreType.DMA((2, STATE)),
             pltpu.VMEM(Wedges.SHAPES[0], F32),
             pltpu.VMEM(Wedges.SHAPES[2], F32),
         ],
         compiler_params=params,
         name="last",
     )(done, own, hist, *edges, *beyond)
-    return out.reshape(perturb.shape)
 
 
 def solution(mesh):

time: 25 us -> 24.5 us (0.980)
  the two profiles are of different devices: /device:TPU:0 before, /device:TPU:2 now
where the time goes in v1:
time: 24.5 us; the launch traced here: 24.4 us
  Pallas kernels  9.13 us (37%)
  starting transfers between devices  8.32 us (34%)
  waiting for transfers between devices  6.15 us (25%)
  between operations  0.7 us (3%)
    ppermute x2, starting transfers between devices, on_device(): lax.ppermute(x, 'lon', swap)  4.56 us
    ppermute x1, starting transfers between devices, rest(): got_fold = lax.ppermute(fold_band, ('lon', 'lat'), across)  3.62 us
    ppermute x2, waiting for transfers between devices, on_device(): lax.ppermute(x, 'lon', swap)  3.48 us
    ppermute x1, waiting for transfers between devices, rest(): lax.ppermute(x, 'lat', swap)  2.67 us
    pallas_call x1, Pallas kernels, on_device(): pl.pallas_call(functools.partial(sides_kernel, sh, sizes), out_shape=(sha...  2.08 us
    pallas_call x1, Pallas kernels, on_device(): pl.pallas_call(functools.partial(last_kernel, sh, sizes), out_shape=jax.S...  1.99 us
    pallas_call x1, Pallas kernels, rest(): done, order, *kept = step_wedges(*got_lat, *got_corners, own, hist, *edges)  1.92 us
    pallas_call x1, Pallas kernels, rest(): edges = step_edges(own, got_a, got_b)  1.19 us
  transfers between devices with their start and end apart: 5, of which 2 were waited for; matrix products, arithmetic and copies ran while one was open for 0% of the time, Pallas kernels for 19%

profile of v1, /device:TPU:2, one launch (start us, length us, event | category | flops | bytes accessed | tf_op | source)
XLA Modules:
  0.0 24.4 jit_solution(8386630676029279406)
XLA Ops:
  0.0 2.1 %sides.1 = (f32[28,8,128]{2,1,0:T(8,128)S(1)}, f32[28,8,128]{2,1,0:T(8,128)S(1)}, f32[4,256,128]{2,1,0:T(8,128)S(1)}, s32[8,128]{1,0:T(8,128)S(1)}, s32[1]{0:T(128)}, /*index=5*/f32[35,8,128]{2,1,0:T(8,128)S(1)}) custom-call(f32[3,256,128]{2,1,0:T(8,128)} %bitcast.2, f32[3,32,128]{2,1,0:T(8,128)} %b_hbm.1, s32[32,128]{1,0:T(8,128)} %m_hbm.1, ...), custom_call_target="tpu_custom_call" | custom-call | tf_op jit(solution)/shard_map/sides/pallas_call | solution.py:885
  2.1 0.1 collective-permute-start.10
  2.2 2.1 %collective-permute-start.8 = (f32[28,8,128]{2,1,0:T(8,128)S(1)}, f32[28,8,128]{2,1,0:T(8,128)S(1)}, u32[]{:S(2)}, u32[]{:S(2)}) collective-permute-start(f32[28,8,128]{2,1,0:T(8,128)S(1)} %get-tuple-element.155), channel_id=1, source_target_pairs={{0,4},{4,0},{8,12},{12,8},{1,5},{5,1},{9,13},{13,9},{2,6},{6,2},{1... | collective-permute-start | bytes 344072 | tf_op jit(solution)/shard_map/ppermute | solution.py:910
  4.3 2.5 %collective-permute-start.9 = (f32[28,8,128]{2,1,0:T(8,128)S(1)}, f32[28,8,128]{2,1,0:T(8,128)S(1)}, u32[]{:S(2)}, u32[]{:S(2)}) collective-permute-start(f32[28,8,128]{2,1,0:T(8,128)S(1)} %get-tuple-element.156), channel_id=1, source_target_pairs={{0,12},{4,8},{8,4},{12,0},{1,13},{5,9},{9,5},{13,1},{2,14},{6,10},... | collective-permute-start | bytes 344072 | tf_op jit(solution)/shard_map/ppermute | solution.py:910
  6.7 0.9 %middle.1.refs_2_ = f32[5,3,256,128]{3,2,1,0:T(8,128)S(1)} custom-call(f32[4,256,128]{2,1,0:T(8,128)S(1)} %get-tuple-element.154.own_ref.refs_1_), custom_call_target="tpu_custom_call" | custom-call | tf_op jit(solution)/shard_map/middle/pallas_call | solution.py:912
  8.3 0.0 collective-permute-done.8.ra_ref
  8.3 3.5 %collective-permute-done.9.rb_ref = f32[28,8,128]{2,1,0:T(8,128)S(1)} collective-permute-done((f32[28,8,128]{2,1,0:T(8,128)S(1)}, f32[28,8,128]{2,1,0:T(8,128)S(1)}, u32[]{:S(2)}, u32[]{:S(2)}) %collective-permute-start.9) | collective-permute-done | bytes 114720 | tf_op jit(solution)/shard_map/ppermute | solution.py:910
  11.8 0.7 %bands.1 = (f32[42,8,128]{2,1,0:T(8,128)S(1)}, f32[7,8,128]{2,1,0:T(8,128)S(1)}) custom-call(f32[4,256,128]{2,1,0:T(8,128)S(1)} %get-tuple-element.154.own_ref.refs_1_, f32[28,8,128]{2,1,0:T(8,128)S(1)} %collective-permute-done.8.ra_ref, f32[28,8,128]{2,1,0:T(8,128)S(1)} %collective-permute-done.9.rb_ref, s32[8,128]{1,0:T(8,128)S(1)} %get-tuple-element.157.place_ref), custom_call_target="tpu_custom_call" | custom-call | tf_op jit(solution)/shard_map/bands/pallas_call | solution.py:922
  12.5 0.0 collective-permute-done.10
  12.5 9.9 %conditional.1 = (f32[3,128,128]{2,1,0:T(8,128)S(1)}, f32[128,128]{1,0:T(8,128)S(1)}, f32[5,3,128,128]{3,2,1,0:T(8,128)S(1)}, f32[3,8,32,128]{3,2,1,0:T(8,128)S(...) conditional(s32[]{:T(128)} %bitcast.1, ...), branch_computations={%region_0.1_spmd, %region_1.2_spmd, %region_2.3_spmd, %region_3.4_... | conditional | bytes 802960 | solution.py:981
  12.6 3.6 %collective-permute-start.7 = (f32[42,8,128]{2,1,0:T(8,128)S(1)}, f32[42,8,128]{2,1,0:T(8,128)S(1)}, u32[]{:S(2)}, u32[]{:S(2)}) collective-permute-start(f32[42,8,128]{2,1,0:T(8,128)S(1)} %get-tuple-element.131), channel_id=1, source_target_pairs={{2,14},{6,10},{10,6},{14,2},{3,15},{7,11},{11,7},{15,3},{18,30},{2... | collective-permute-start | bytes 516104 | tf_op jit(solution)/shard_map/cond/branch_3_fun/ppermute | solution.py:975
  16.2 0.1 collective-permute-start.6
  16.3 1.2 %edges.7 = (f32[3,128,128]{2,1,0:T(8,128)S(1)}, f32[128,128]{1,0:T(8,128)S(1)}, f32[5,3,128,128]{3,2,1,0:T(8,128)S(1)}) custom-call(f32[4,256,128]{2,1,0:T(8,128)S(1)} %get-tuple-element.120.own_ref.refs_2_, f32[28,8,128]{2,1,0:T(8,128)S(1)} %get-tuple-element.122.ra_ref, f32[28,8,128]{2,1,0:T(8,128)S(1)} %get-tuple-element.123.rb_ref), custom_call_target="tpu_custom_call" | custom-call | tf_op jit(solution)/shard_map/cond/branch_3_fun/jit(wrapped)/edges/pallas_call | solution.py:977
  17.5 2.7 %collective-permute-done.6.refs_1_ = f32[7,8,128]{2,1,0:T(8,128)S(1)} collective-permute-done((f32[7,8,128]{2,1,0:T(8,128)S(1)}, f32[7,8,128]{2,1,0:T(8,128)S(1)}, u32[]{:S(2)}, u32[]{:S(2)}) %collective-permute-start.6) | collective-permute-done | bytes 28704 | tf_op jit(solution)/shard_map/cond/branch_3_fun/ppermute | solution.py:976
  20.1 1.9 %wedges.7 = (f32[3,8,32,128]{3,2,1,0:T(8,128)S(1)}, f32[8,128]{1,0:T(8,128)S(1)}, f32[3,128,128]{2,1,0:T(8,128)S(1)}, f32[128,128]{1,0:T(8,128)S(1)}, f32[5,3,128,128]{3,2,1,0:T(8,128)S(1)}) custom-call(f32[35,8,128]{2,1,0:T(8,128)S(1)} %get-tuple-element.118.refs_0_, f32[7,8,128]{2,1,0:T(8,128)S(1)} %collective-permute-done.6.refs_1_, ...), custom_call_target="tpu_custom_call" | custom-call | tf_op jit(solution)/shard_map/cond/branch_3_fun/jit(wrapped)/wedges/pallas_call | solution.py:978
  22.0 0.0 collective-permute-done.7.fold_ref
  22.1 0.3 %north.7 = (f32[3,320,128]{2,1,0:T(8,128)S(1)}, f32[320,128]{1,0:T(8,128)S(1)}, f32[4,160,128]{2,1,0:T(8,128)S(1)}, f32[80,128]{1,0:T(8,128)S(1)}) custom-call(f32[42,8,128]{2,1,0:T(8,128)S(1)} %collective-permute-done.7.fold_ref, f32[8,128]{1,0:T(8,128)S(1)} %get-tuple-element.132.order_ref), custom_call_target="tpu_custom_call" | custom-call | tf_op jit(solution)/shard_map/cond/branch_3_fun/jit(wrapped)/north/pallas_call | solution.py:979
  22.4 2.0 %last.1 = f32[3,8,32,128]{3,2,1,0:T(8,128)} custom-call(f32[3,8,32,128]{3,2,1,0:T(8,128)S(1)} %get-tuple-element.161.refs_0_, f32[4,256,128]{2,1,0:T(8,128)S(1)} %get-tuple-element.154.own_ref.refs_1_, f32[5,3,256,128]{3,2,1,0:T(8,128)S(1)} %middle.1.refs_2_, f32[3,128,128]{2,1,0:T(8,128)S(1)} %get-tuple-element.162.refs_3_, ...), custom_call_target="tpu_custom_call" | custom-call | tf_op jit(solution)/shard_map/last/pallas_call | solution.py:992
Async XLA Ops:
  2.1 10.4 %collective-permute-start.10 = (f32[35,8,128]{2,1,0:T(8,128)S(1)}, f32[35,8,128]{2,1,0:T(8,128)S(1)}, u32[]{:S(2)}, u32[]{:S(2)}) collective-permute-start(f32[35,8,128]{2,1,0:T(8,128)S(1)} %get-tuple-element.159), channel_id=1, source_target_pairs={{0,2},{2,0},{1,3},{3,1},{4,6},{6,4},{5,7},{7,5},{8,10},{10,8},{9,1... | collective-permute-start | bytes 430088 | tf_op jit(solution)/shard_map/ppermute | solution.py:921
  2.2 6.2 %collective-permute-start.8 = (f32[28,8,128]{2,1,0:T(8,128)S(1)}, f32[28,8,128]{2,1,0:T(8,128)S(1)}, u32[]{:S(2)}, u32[]{:S(2)}) collective-permute-start(f32[28,8,128]{2,1,0:T(8,128)S(1)} %get-tuple-element.155), channel_id=1, source_target_pairs={{0,4},{4,0},{8,12},{12,8},{1,5},{5,1},{9,13},{13,9},{2,6},{6,2},{1... | collective-permute-start | bytes 344072 | tf_op jit(solution)/shard_map/ppermute | solution.py:910
  4.3 7.6 %collective-permute-start.9 = (f32[28,8,128]{2,1,0:T(8,128)S(1)}, f32[28,8,128]{2,1,0:T(8,128)S(1)}, u32[]{:S(2)}, u32[]{:S(2)}) collective-permute-start(f32[28,8,128]{2,1,0:T(8,128)S(1)} %get-tuple-element.156), channel_id=1, source_target_pairs={{0,12},{4,8},{8,4},{12,0},{1,13},{5,9},{9,5},{13,1},{2,14},{6,10},... | collective-permute-start | bytes 344072 | tf_op jit(solution)/shard_map/ppermute | solution.py:910
  12.6 9.5 %collective-permute-start.7 = (f32[42,8,128]{2,1,0:T(8,128)S(1)}, f32[42,8,128]{2,1,0:T(8,128)S(1)}, u32[]{:S(2)}, u32[]{:S(2)}) collective-permute-start(f32[42,8,128]{2,1,0:T(8,128)S(1)} %get-tuple-element.131), channel_id=1, source_target_pairs={{2,14},{6,10},{10,6},{14,2},{3,15},{7,11},{11,7},{15,3},{18,30},{2... | collective-permute-start | bytes 516104 | tf_op jit(solution)/shard_map/cond/branch_3_fun/ppermute | solution.py:975
  16.2 3.9 %collective-permute-start.6 = (f32[7,8,128]{2,1,0:T(8,128)S(1)}, f32[7,8,128]{2,1,0:T(8,128)S(1)}, u32[]{:S(2)}, u32[]{:S(2)}) collective-permute-start(f32[7,8,128]{2,1,0:T(8,128)S(1)} %get-tuple-element.119), channel_id=1, source_target_pairs={{0,2},{2,0},{1,3},{3,1},{4,6},{6,4},{5,7},{7,5},{8,10},{10,8},{9,1... | collective-permute-start | bytes 86024 | tf_op jit(solution)/shard_map/cond/branch_3_fun/ppermute | solution.py:976

commit v2 on v1

--- a/solution.py
+++ b/solution.py
@@ -164,24 +164,22 @@
             raw_rows(outs[1], top)
 
 
-def sides_kernel(sh, sizes, x_hbm, b_hbm, m_hbm, l_hbm, p_hbm, *rest):
-    a_out, b_out, own_ref, place_out, q_out = rest[:5]
-    lat_outs, (x_ref, b_ref, m_ref, l_ref, p_ref, sems) = rest[5:-6], rest[-6:]
-    lat_size, lon_size = sizes
+def sides_kernel(sh, sizes, x_hbm, b_hbm, m_hbm, l_hbm, *rest):
+    a_out, b_out, own_ref = rest[:3]
+    lat_outs, (x_ref, b_ref, m_ref, l_ref, sems) = rest[3:-5], rest[-5:]
+    lat_size, _ = sizes
     height = sh.height
     copies = [
         pltpu.make_async_copy(src, dst, sems.at[n])
         for n, (src, dst) in enumerate(
-            [(b_hbm, b_ref), (m_hbm, m_ref), (l_hbm, l_ref), (p_hbm, p_ref)]
+            [(b_hbm, b_ref), (m_hbm, m_ref), (l_hbm, l_ref)]
             + [(x_hbm.at[f], x_ref.at[f]) for f in range(STATE)]
         )
     ]
     for copy in copies:
         copy.start()
-    for copy in copies[:4]:
+    for copy in copies[:3]:
         copy.wait()
-    q_out[0], place = fold_place(p_ref, lon_size)
-    place_out[...] = jnp.full((SUBLANES, LANES), place, jnp.int32)
 
     wet = m_ref[...].astype(F32)
     depth = 0.5 + 1.5 * ((l_ref[...] - 1).astype(F32) / (NLEV - 1)) ** 2
@@ -201,7 +199,7 @@
             own_ref[COEF, pl.ds(SUBLANES * r + c, SUBLANES, stride=SUBLANES), :] = plane[
                 r : r + SUBLANES
             ]
-    for copy in copies[4:]:
+    for copy in copies[3:]:
         copy.wait()
     for f in range(STATE):
         for r in range(height):
@@ -400,7 +398,7 @@
         self.flux_n, self.rolled, self.new, self.slopes = {}, {}, {}, {}
         self.sign = HALF_STEP * north_sign() if mirror is not None else HALF_STEP
         self.first = min(elev[0] - 1, vel[0])
-        self.last = (max(elev[1] + 1, vel[1]) if mirror is None else mirror) + 2 * LAG
+        self.last = max(elev[1], vel[1]) + 2 * LAG
 
     def flux(self, r):
         lo, hi = self.elev_rows
@@ -459,31 +457,42 @@
         self.velocity(t - 2 * LAG)
 
 
-def run_sweeps(sweeps):
-    for t in range(max(s.last - s.first for s in sweeps) + 1):
-        for s in sweeps:
-            s.advance(s.first + t)
-
-
-def middle_kernel(sh, own_ref, hist_ref):
+def run_chains(chains):
+    starts = []
+    for chain in chains:
+        at, ticks = 0, []
+        for n, sweep in enumerate(chain):
+            if n:
+                at += max(2 * LAG + sweep.first - chain[n - 1].first, 0)
+            ticks.append(at)
+        starts.append(ticks)
+    ends = [ticks[n] + s.last - s.first for c, ticks in zip(chains, starts) for n, s in enumerate(c)]
+    for t in range(max(ends) + 1):
+        for n in range(SUBCYCLES):
+            for chain, ticks in zip(chains, starts):
+                if t >= ticks[n]:
+                    chain[n].advance(chain[n].first + t - ticks[n])
+
+
+def middle_kernel(sh, sizes, own_ref, p_hbm, hist_ref, place_out, q_out, p_ref, sem):
+    copy = pltpu.make_async_copy(p_hbm, p_ref, sem)
+    copy.start()
+    chain = []
     for step in range(1, SUBCYCLES + 1):
-        before, after = hist_ref.at[max(step - 2, 0)], hist_ref.at[step - 1]
-        source = own_ref if step == 1 else before
-
-        def put(f, r, value, after=after):
-            put_row(after, f, r, value)
-
-        run_sweeps(
-            [
-                Sweep(
-                    (2 * step - 1, sh.height - 2 * step + 1),
-                    (2 * step, sh.height - 2 * step),
-                    functools.partial(row, source),
-                    functools.partial(coef, own_ref.at[COEF]),
-                    put,
-                )
-            ]
+        source = own_ref if step == 1 else hist_ref.at[step - 2]
+        chain.append(
+            Sweep(
+                (2 * step - 1, sh.height - 2 * step + 1),
+                (2 * step, sh.height - 2 * step),
+                functools.partial(row, source),
+                functools.partial(coef, own_ref.at[COEF]),
+                functools.partial(put_row, hist_ref.at[step - 1]),
+            )
         )
+    run_chains([chain])
+    copy.wait()
+    q_out[0], place = fold_place(p_ref, sizes[1])
+    place_out[...] = jnp.full((SUBLANES, LANES), place, jnp.int32)
 
 
 def edges_kernel(sh, own_ref, ra_ref, rb_ref, start_ref, coef_ref, hist_ref):
@@ -527,25 +536,20 @@
     run_staged([edge_row(f, k) for k in range(HALO, sh.mid) for f in range(FIELDS)], 4)
 
     rows = sh.mid - HALO
+    chain = []
     for step in range(1, SUBCYCLES + 1):
         source = start_ref if step == 1 else hist_ref.at[step - 2]
-        after = hist_ref.at[step - 1]
-
-        def put(f, r, value, after=after):
-            put_row(after, f, r, value)
-
-        run_sweeps(
-            [
-                Sweep(
-                    (2 * step - 1, rows),
-                    (2 * step, rows),
-                    functools.partial(row, source),
-                    functools.partial(coef, coef_ref),
-                    put,
-                    mirror=rows,
-                )
-            ]
+        chain.append(
+            Sweep(
+                (2 * step - 1, rows),
+                (2 * step, rows),
+                functools.partial(row, source),
+                functools.partial(coef, coef_ref),
+                functools.partial(put_row, hist_ref.at[step - 1]),
+                mirror=rows,
+            )
         )
+    run_chains([chain])
 
 
 def own_columns(a, b):
@@ -569,15 +573,17 @@
 
 
 class Wedges:
-    def __init__(self, sh, own_ref, hist_ref, start_ref, ecoef_ref, ehist_ref, buffers):
-        self.sh, self.own, self.hist = sh, own_ref, hist_ref
-        self.start, self.ecoef, self.ehist = start_ref, ecoef_ref, ehist_ref
-        self.main, self.main_c, self.edge, self.edge_c = buffers
+    def __init__(self, sh, own=None, hist=None, edges=(None,) * 3, main=None, edge=None):
+        self.sh, self.own, self.hist = sh, own, hist
+        self.start, self.ecoef, self.ehist = edges
+        self.main, self.begin, self.main_c = main
+        self.edge, self.edge_c = edge or (None, None)
         lane = lane_ids()
         self.low = lane < HALF
         self.half_lane = half = lane & (HALF - 1)
         self.east_own = (half >= EAST0) & (half < EAST0 + 2 * HALO)
-        self.halo = (half < HALO) | ((half >= EAST0 + 2 * HALO) & (half < EAST0 + 3 * HALO))
+        halo = (half < HALO) | ((half >= EAST0 + 2 * HALO) & (half < EAST0 + 3 * HALO))
+        self.halo_south, self.halo_north = halo & self.low, halo & (lane >= HALF)
         self.sign = north_sign()
 
     SHAPES = (
@@ -596,6 +602,9 @@
             at = SUBLANES * self.at(r)
             return self.main_c[at : at + SUBLANES, :]
         return row(self.main, f, self.at(r))
+
+    def first_row(self, f, r):
+        return self.main_row(f, r) if f == COEF else row(self.begin, f, self.at(r))
 
     def put_main(self, f, r, value):
         if f < STATE:
@@ -607,48 +616,56 @@
 
     def put_halo(self, f, r, value):
         north = r >= self.sh.mid
-        k, base = (self.sh.ext - 1 - r, HALF) if north else (r, 0)
-        self.edge[f, SUBLANES * k : SUBLANES * (k + 1), base : base + HALF] = value[
-            :, base : base + HALF
-        ]
-
-    def take_band(self, ref, halos, north):
-        def band_row(f, i):
-            r = self.sh.ext - HALO + i if north else i
-            if f < STATE:
-                value = ref[f * HALO + i]
-            else:
-                value = ref[STATE * HALO + i % PAIRS]
-                value = value if i < PAIRS else roll(value, SUBLANES // 2, 0)
-            w, e = halos(f, i, HALF if north else 0)
+        k, mask = (self.sh.ext - 1 - r, self.halo_north) if north else (r, self.halo_south)
+        put_row(self.edge, f, k, jnp.where(mask, value, row(self.edge, f, k)))
+
+    def band(self, north):
+        return [self.sh.ext - HALO + i if north else i for i in range(HALO)]
+
+    def take_rows(self, ref, north):
+        for f in range(FIELDS):
+            for i, r in enumerate(self.band(north)):
+                if ref is None:
+                    value = jnp.zeros((SUBLANES, LANES), F32)
+                elif f < STATE:
+                    value = ref[f * HALO + i]
+                else:
+                    value = ref[STATE * HALO + i % PAIRS]
+                    value = value if i < PAIRS else roll(value, SUBLANES // 2, 0)
+                self.put_main(f, r, value)
+                if f < STATE and self.begin is not self.main:
+                    put_row(self.begin, f, self.at(r), value)
+
+    def take_halos(self, ref, first, north):
+        base = HALF if north else 0
+        if ref is None:
+            for f in range(FIELDS):
+                for r in self.band(north):
+                    self.put_halo(f, r, jnp.zeros((SUBLANES, LANES), F32))
+            return
+
+        def band_row(f, i, r):
+            v, at = self.sh.corner(i, f)
+            v = ref[v - self.sh.main + first]
+            w, e = roll(v, base - at), roll(v, base + EAST0 + HALO - at)
             yield
-            self.put_main(f, r, value)
             self.put_halo(f, r, jnp.where(self.half_lane < HALO, w, e))
 
-        run_staged([band_row(f, i) for f in range(FIELDS) for i in range(HALO)], 10)
-
-    def no_band(self, north):
-        zero = jnp.zeros((SUBLANES, LANES), F32)
-        for f in range(FIELDS):
-            for i in range(HALO):
-                r = self.sh.ext - HALO + i if north else i
-                self.put_main(f, r, zero)
-                self.put_halo(f, r, zero)
-
-    def edge_rows(self, north_only=False):
+        rows = list(enumerate(self.band(north)))
+        run_staged([band_row(f, i, r) for f in range(FIELDS) for i, r in rows], 16)
+
+    def edge_own(self, out, north_only=False):
         def edge_row(f, k):
-            b = self.main_row(f, self.sh.ext - 1 - k)
-            parts = own_columns(b if north_only else self.main_row(f, k), b)
+            b = self.first_row(f, self.sh.ext - 1 - k)
+            parts = own_columns(b if north_only else self.first_row(f, k), b)
             yield
-            value = jnp.where(
-                self.halo, row(self.edge, f, k), merge_own(parts, self.low, self.east_own)
-            )
-            if f == COEF:
-                put_edge_coefs(self.edge_c, k, value, self.sign)
-            else:
-                put_row(self.edge, f, k, value)
+            put_row(out, f, k, merge_own(parts, self.low, self.east_own))
 
         run_staged([edge_row(f, k) for k in range(HALO) for f in range(FIELDS)], 8)
+
+    def edge_coefs(self):
+        for k in range(HALO):
+            put_edge_coefs(self.edge_c, k, row(self.edge, COEF, k), self.sign)
 
     def steps(self, sides):
         ext = self.sh.ext
@@ -664,36 +681,35 @@
                 return coef(self.own.at[COEF], r - HALO, c)
             return coef(self.main_c, self.at(r), c)
 
+        edges, south, north = [], [], []
         for step in range(1, SUBCYCLES + 1):
-            source = self.own if step == 1 else self.hist.at[step - 2]
-            e_source = self.start if step == 1 else self.ehist.at[step - 2]
-            after, e_after = self.hist.at[step - 1], self.ehist.at[step - 1]
             first, ready = 2 * step - 2, 2 * step + HALO - 2
 
-            def old_main(f, r, source=source, ready=ready):
+            def old_main(f, r, step=step, ready=ready):
                 if ready <= r < ext - ready:
-                    return row(source, f, r - HALO)
+                    return row(self.own if step == 1 else self.hist.at[step - 2], f, r - HALO)
                 return self.main_row(f, r)
 
-            def old_edge(f, k, e_source=e_source, ready=ready):
-                return row(e_source, f, k - HALO) if k >= ready else row(self.edge, f, k)
-
-            def known_main(r, after=after):
-                return row(after, 0, r - HALO)
-
-            def known_edge(k, e_after=e_after):
-                return row(e_after, 0, k - HALO)
+            def old_edge(f, k, step=step, ready=ready):
+                if k >= ready:
+                    return row(self.start if step == 1 else self.ehist.at[step - 2], f, k - HALO)
+                return row(self.edge, f, k)
+
+            def known_main(r, step=step):
+                return row(self.hist.at[step - 1], 0, r - HALO)
+
+            def known_edge(k, step=step):
+                return row(self.ehist.at[step - 1], 0, k - HALO)
 
             elev, vel = (first + 1, ready + 1), (first + 2, ready + 2)
-            sweeps = [
+            edges.append(
                 Sweep(elev, vel, old_edge, edge_coef, put_edge, known_edge, mirror=self.sh.mid)
-            ]
-            if "south" in sides:
-                sweeps.append(Sweep(elev, vel, old_main, main_coef, self.put_main, known_main))
-            if "north" in sides:
-                elev, vel = [(ext - rows[1], ext - rows[0]) for rows in (elev, vel)]
-                sweeps.append(Sweep(elev, vel, old_main, main_coef, self.put_main, known_main))
-            run_sweeps(sweeps)
+            )
+            south.append(Sweep(elev, vel, old_main, main_coef, self.put_main, known_main))
+            elev, vel = [(ext - rows[1], ext - rows[0]) for rows in (elev, vel)]
+            north.append(Sweep(elev, vel, old_main, main_coef, self.put_main, known_main))
+        chains = {"edges": edges, "south": south, "north": north}
+        run_chains([chains[name] for name in sides])
 
     def output(self, first, last, put):
         ext, mid, ready = self.sh.ext, self.sh.mid, 2 * HALO
@@ -713,59 +729,53 @@
         run_staged([output_row(f, r) for f in range(STATE) for r in range(first, last)], 10)
 
 
-def wedge_kernel(sh, sizes, n_lat, *refs):
+def for_bands(sizes, n_lat, take):
     lat_size, _ = sizes
-    bands, refs = [(refs[n], refs[n_lat + n]) for n in range(n_lat)], refs[2 * n_lat :]
-    state, (out_ref, order_out), kept, buffers = refs[:5], refs[5:7], refs[7:10], refs[10:]
-    wedges = Wedges(sh, *state, buffers)
-    order_out[...] = jnp.zeros((SUBLANES, LANES), F32)
-    for source, target in zip(state[2:], kept):
-        target[...] = source[...]
-
-    def take(band, north):
-        ref, corners = band
-
-        def halos(f, i, base):
-            v, at = sh.corner(i, f)
-            v = corners[v - sh.main]
-            return roll(v, base - at), roll(v, base + EAST0 + HALO - at)
-
-        wedges.take_band(ref, halos, north)
-
     lat = lax.axis_index("lat")
     lat_even = lax.rem(lat, 2) == 0
     lat_odd = jnp.logical_not(lat_even)
     at_top = lat == lat_size - 1
-
-    @pl.when(at_top)
-    def _():
-        wedges.no_band(True)
-
-    @pl.when(lat == 0)
-    def _():
-        wedges.no_band(False)
-
-    @pl.when(lat_even)
-    def _():
-        take(bands[0], True)
-
-    @pl.when(lat_odd)
-    def _():
-        take(bands[0], False)
-
+    pl.when(at_top)(lambda: take(None, True))
+    pl.when(lat == 0)(lambda: take(None, False))
+    pl.when(lat_even)(lambda: take(0, True))
+    pl.when(lat_odd)(lambda: take(0, False))
     if n_lat == 2:
-
-        @pl.when(lat_odd & jnp.logical_not(at_top))
-        def _():
-            take(bands[1], True)
-
-        @pl.when(lat_even & (lat > 0))
-        def _():
-            take(bands[1], False)
-
-    wedges.edge_rows()
+        pl.when(lat_odd & jnp.logical_not(at_top))(lambda: take(1, True))
+        pl.when(lat_even & (lat > 0))(lambda: take(1, False))
+
+
+def wedge_rows_kernel(sh, sizes, n_lat, *refs):
+    bands, edges, outs = refs[:n_lat], refs[-10:-7], refs[-7:]
+    own_ref, hist_ref = refs[n_lat], refs[n_lat + 1]
+    main, edge_out, kept = outs[:3], outs[3], outs[4:]
+    wedges = Wedges(sh, own_ref, hist_ref, main=main)
+
+    def take(n, north):
+        wedges.take_rows(None if n is None else bands[n], north)
+
+    for_bands(sizes, n_lat, take)
+    wedges.edge_own(edge_out)
+    for source, target in zip(edges, kept):
+        target[...] = source[...]
     wedges.steps(("south", "north"))
 
+
+def wedge_edges_kernel(sh, sizes, n_lat, *refs):
+    corners, refs = refs[:n_lat], refs[n_lat:]
+    hist_ref, main, edge_own, edges = refs[0], refs[1], refs[2], refs[3:6]
+    out_ref, order_out, *edge = refs[6:]
+    wedges = Wedges(sh, None, hist_ref, edges, (main, None, None), edge)
+    order_out[...] = jnp.zeros((SUBLANES, LANES), F32)
+    for f in range(FIELDS):
+        for k in range(HALO):
+            put_row(edge[0], f, k, row(edge_own, f, k))
+
+    def take(n, north):
+        wedges.take_halos(None if n is None else corners[n], 0, north)
+
+    for_bands(sizes, n_lat, take)
+    wedges.edge_coefs()
+    wedges.steps(("edges",))
     out_flat = flat_rows(out_ref)
 
     def put(f, r, value):
@@ -774,18 +784,14 @@
     wedges.output(HALO, sh.ext - HALO, put)
 
 
-def north_kernel(sh, sizes, fold_ref, order_ref, *buffers):
+def north_kernel(sh, sizes, fold_ref, order_ref, main, main_c, edge, edge_c):
     @pl.when(lax.axis_index("lat") == sizes[0] - 1)
     def _():
-        wedges = Wedges(sh, None, None, None, None, None, buffers)
-        wedges.no_band(False)
-
-        def halos(f, i, base):
-            v, at = sh.corner(i, f)
-            return roll(fold_ref[v], base - at), roll(fold_ref[v], base + EAST0 + HALO - at)
-
-        wedges.take_band(fold_ref, halos, True)
-        wedges.edge_rows(north_only=True)
+        wedges = Wedges(sh, main=(main, main, main_c), edge=(edge, edge_c))
+        wedges.take_rows(fold_ref, True)
+        wedges.edge_own(edge, north_only=True)
+        wedges.take_halos(fold_ref, sh.main, True)
+        wedges.edge_coefs()
 
 
 def last_kernel(sh, sizes, *refs):
@@ -819,13 +825,15 @@
 
     @pl.when(at_top)
     def _():
-        wedges = Wedges(sh, *state, (main, begin[1], edge, begin[3]))
+        wedges = Wedges(
+            sh, *state[:2], state[2:], (main, main, begin[1]), (edge, begin[3])
+        )
         for f in range(STATE):
             for k in range(HALO):
                 put_row(edge, f, k, row(begin[2], f, k))
                 at = wedges.at(ext - 1 - k)
                 put_row(main, f, at, row(begin[0], f, at))
-        wedges.steps(("north",))
+        wedges.steps(("edges", "north"))
 
         late_flat, done_flat = flat_rows(late_ref), flat_rows(done_ref)
 
@@ -882,41 +890,46 @@
     params = pltpu.CompilerParams(vmem_limit_bytes=16 * 1024 * 1024)
     rows = SUBLANES * height
     n_lat = 1 if lat_size == 2 else 2
-    side_a, side_b, own, place, branch, *lat_out = pl.pallas_call(
+    side_a, side_b, own, *lat_out = pl.pallas_call(
         functools.partial(sides_kernel, sh, sizes),
         out_shape=(
             shape(sh.side),
             shape(sh.side),
             pltpu.VMEM((FIELDS, rows, LANES), F32),
-            pltpu.VMEM(tile, jnp.int32),
-            jax.ShapeDtypeStruct((1,), jnp.int32),
         )
         + (shape(sh.main),) * n_lat,
-        in_specs=[pl.BlockSpec(memory_space=pltpu.HBM)] * 5,
-        out_specs=tuple(vmem(4)) + (smem(),) + tuple(vmem(n_lat)),
+        in_specs=[pl.BlockSpec(memory_space=pltpu.HBM)] * 4,
+        out_specs=tuple(vmem(3 + n_lat)),
         scratch_shapes=[
             pltpu.VMEM(flat.shape, F32),
             pltpu.VMEM(background.shape, F32),
             pltpu.VMEM(land_mask.shape, jnp.int32),
             pltpu.VMEM(levels.shape, jnp.int32),
-            pltpu.SMEM(fold_partner.shape, jnp.int32),
-            pltpu.SemaphoreType.DMA((4 + STATE,)),
+            pltpu.SemaphoreType.DMA((3 + STATE,)),
         ],
         compiler_params=params,
         name="sides",
-    )(*[in_hbm(v) for v in (flat, background, land_mask, levels, fold_partner)])
+    )(*[in_hbm(v) for v in (flat, background, land_mask, levels)])
 
     lon_swaps = pair_swaps(lon_size, True)
     got_a, got_b = [lax.ppermute(x, "lon", swap) for x, swap in zip((side_a, side_b), lon_swaps)]
 
-    hist = pl.pallas_call(
-        functools.partial(middle_kernel, sh),
-        out_shape=pltpu.VMEM((SUBCYCLES, STATE, rows, LANES), F32),
-        in_specs=vmem(1),
-        out_specs=vmem(1)[0],
+    hist, place, branch = pl.pallas_call(
+        functools.partial(middle_kernel, sh, sizes),
+        out_shape=(
+            pltpu.VMEM((SUBCYCLES, STATE, rows, LANES), F32),
+            pltpu.VMEM(tile, jnp.int32),
+            jax.ShapeDtypeStruct((1,), jnp.int32),
+        ),
+        in_specs=vmem(1) + [pl.BlockSpec(memory_space=pltpu.HBM)],
+        out_specs=tuple(vmem(2)) + (smem(),),
+        scratch_shapes=[
+            pltpu.SMEM(fold_partner.shape, jnp.int32),
+            pltpu.SemaphoreType.DMA,
+        ],
         compiler_params=params,
         name="middle",
-    )(own)
+    )(own, in_hbm(fold_partner))
     lat_swaps = pair_swaps(lat_size, False)[:n_lat]
     got_lat = [lax.ppermute(x, "lat", swap) for x, swap in zip(lat_out, lat_swaps)]
     fold_band, *lat_corners = pl.pallas_call(
@@ -944,15 +957,25 @@
             name="edges",
         )
     )
-    step_wedges = jax.jit(
+    step_wedge_rows = jax.jit(
         pl.pallas_call(
-            functools.partial(wedge_kernel, sh, sizes, n_lat),
-            out_shape=(pltpu.VMEM(perturb.shape, F32), pltpu.VMEM(tile, F32)) + edge_shapes,
-            in_specs=vmem(2 * n_lat + 5),
-            out_specs=tuple(vmem(5)),
-            scratch_shapes=[pltpu.VMEM(x, F32) for x in Wedges.SHAPES],
+            functools.partial(wedge_rows_kernel, sh, sizes, n_lat),
+            out_shape=tuple(pltpu.VMEM(Wedges.SHAPES[n], F32) for n in (0, 0, 1, 2)) + edge_shapes,
+            in_specs=vmem(n_lat + 5),
+            out_specs=tuple(vmem(7)),
             compiler_params=params,
-            name="wedges",
+            name="wedge_rows",
+        )
+    )
+    step_wedge_edges = jax.jit(
+        pl.pallas_call(
+            functools.partial(wedge_edges_kernel, sh, sizes, n_lat),
+            out_shape=(pltpu.VMEM(perturb.shape, F32), pltpu.VMEM(tile, F32)),
+            in_specs=vmem(n_lat + 6),
+            out_specs=tuple(vmem(2)),
+            scratch_shapes=[pltpu.VMEM(x, F32) for x in Wedges.SHAPES[2:]],
+            compiler_params=params,
+            name="wedge_edges",
         )
     )
     take_north = jax.jit(
@@ -975,7 +998,8 @@
         got_fold = lax.ppermute(fold_band, ("lon", "lat"), across)
         got_corners = [lax.ppermute(x, "lat", swap) for x, swap in zip(lat_corners, lat_swaps)]
         edges = step_edges(own, got_a, got_b)
-        done, order, *kept = step_wedges(*got_lat, *got_corners, own, hist, *edges)
+        main, _, _, edge_own, *kept = step_wedge_rows(*got_lat, own, hist, *edges)
+        done, order = step_wedge_edges(*got_corners, hist, main, edge_own, *edges)
         return kept, done, take_north(got_fold, order)
 
     edges, done, beyond = lax.switch(

time: 24.5 us -> 22.1 us (0.902)
  the two profiles are of different devices: /device:TPU:2 before, /device:TPU:10 now
where the time goes in v2:
time: 22.1 us; the launch traced here: 21.9 us
  Pallas kernels  10.1 us (46%)
  starting transfers between devices  7.37 us (33%)
  waiting for transfers between devices  3.66 us (17%)
  between operations  0.7 us (3%)
    ppermute x1, starting transfers between devices, rest(): got_fold = lax.ppermute(fold_band, ('lon', 'lat'), across)  3.56 us
    ppermute x2, starting transfers between devices, on_device(): lax.ppermute(x, 'lon', swap)  3.15 us
    ppermute x2, waiting for transfers between devices, on_device(): lax.ppermute(x, 'lon', swap)  2.88 us
    pallas_call x1, Pallas kernels, on_device(): pl.pallas_call(functools.partial(last_kernel, sh, sizes), out_shape=jax.S...  1.94 us
    pallas_call x1, Pallas kernels, rest(): main, _, _, edge_own, *kept = step_wedge_rows(*got_lat, own, hist, *edges)  1.89 us
    pallas_call x1, Pallas kernels, on_device(): pl.pallas_call(functools.partial(sides_kernel, sh, sizes), out_shape=(sha...  1.56 us
    pallas_call x1, Pallas kernels, on_device(): pl.pallas_call(functools.partial(middle_kernel, sh, sizes), out_shape=(pl...  1.49 us
    pallas_call x1, Pallas kernels, rest(): edges = step_edges(own, got_a, got_b)  1.18 us
  transfers between devices with their start and end apart: 5, of which 2 were waited for; matrix products, arithmetic and copies ran while one was open for 0% of the time, Pallas kernels for 29%

profile of v2, /device:TPU:10, one launch (start us, length us, event | category | flops | bytes accessed | tf_op | source)
XLA Modules:
  0.0 21.9 jit_solution(275717893918291634)
XLA Ops:
  0.0 1.6 %sides.1 = (f32[28,8,128]{2,1,0:T(8,128)S(1)}, f32[28,8,128]{2,1,0:T(8,128)S(1)}, f32[4,256,128]{2,1,0:T(8,128)S(1)}, f32[35,8,128]{2,1,0:T(8,128)S(1)}) custom-call(f32[3,256,128]{2,1,0:T(8,128)} %bitcast.2, f32[3,32,128]{2,1,0:T(8,128)} %b_hbm.1, s32[32,128]{1,0:T(8,128)} %m_hbm.1, s32[32,128]{1,0:T(8,128)} %l_hbm.1), custom_call_target="tpu_custom_call" | custom-call | tf_op jit(solution)/shard_map/sides/pallas_call | solution.py:893
  1.6 0.6 %collective-permute-start.10 = (f32[35,8,128]{2,1,0:T(8,128)S(1)}, f32[35,8,128]{2,1,0:T(8,128)S(1)}, u32[]{:S(2)}, u32[]{:S(2)}) collective-permute-start(f32[35,8,128]{2,1,0:T(8,128)S(1)} %get-tuple-element.166), channel_id=1, source_target_pairs={{0,2},{2,0},{1,3},{3,1},{4,6},{6,4},{5,7},{7,5},{8,10},{10,8},{9,1... | collective-permute-start | bytes 430088 | tf_op jit(solution)/shard_map/ppermute | solution.py:934
  2.2 0.0 collective-permute-start.8
  2.2 3.1 %collective-permute-start.9 = (f32[28,8,128]{2,1,0:T(8,128)S(1)}, f32[28,8,128]{2,1,0:T(8,128)S(1)}, u32[]{:S(2)}, u32[]{:S(2)}) collective-permute-start(f32[28,8,128]{2,1,0:T(8,128)S(1)} %get-tuple-element.165), channel_id=1, source_target_pairs={{0,12},{4,8},{8,4},{12,0},{1,13},{5,9},{9,5},{13,1},{2,14},{6,10},... | collective-permute-start | bytes 344072 | tf_op jit(solution)/shard_map/ppermute | solution.py:915
  5.3 1.5 %middle.1 = (f32[5,3,256,128]{3,2,1,0:T(8,128)S(1)}, s32[8,128]{1,0:T(8,128)S(1)}, s32[1]{0:T(128)}) custom-call(f32[4,256,128]{2,1,0:T(8,128)S(1)} %get-tuple-element.162.own_ref.refs_1_, s32[512]{0:T(512)} %p_hbm.1), custom_call_target="tpu_custom_call" | custom-call | tf_op jit(solution)/shard_map/middle/pallas_call | solution.py:917
  7.5 0.0 collective-permute-done.8.ra_ref
  7.5 2.9 %collective-permute-done.9.rb_ref = f32[28,8,128]{2,1,0:T(8,128)S(1)} collective-permute-done((f32[28,8,128]{2,1,0:T(8,128)S(1)}, f32[28,8,128]{2,1,0:T(8,128)S(1)}, u32[]{:S(2)}, u32[]{:S(2)}) %collective-permute-start.9) | collective-permute-done | bytes 114720 | tf_op jit(solution)/shard_map/ppermute | solution.py:915
  10.3 0.7 %bands.1 = (f32[42,8,128]{2,1,0:T(8,128)S(1)}, f32[7,8,128]{2,1,0:T(8,128)S(1)}) custom-call(f32[4,256,128]{2,1,0:T(8,128)S(1)} %get-tuple-element.162.own_ref.refs_1_, f32[28,8,128]{2,1,0:T(8,128)S(1)} %collective-permute-done.8.ra_ref, f32[28,8,128]{2,1,0:T(8,128)S(1)} %collective-permute-done.9.rb_ref, s32[8,128]{1,0:T(8,128)S(1)} %get-tuple-element.168.place_ref), custom_call_target="tpu_custom_call" | custom-call | tf_op jit(solution)/shard_map/bands/pallas_call | solution.py:935
  11.0 0.0 collective-permute-done.10
  11.0 8.9 %conditional.1 = (f32[3,128,128]{2,1,0:T(8,128)S(1)}, f32[128,128]{1,0:T(8,128)S(1)}, f32[5,3,128,128]{3,2,1,0:T(8,128)S(1)}, f32[3,8,32,128]{3,2,1,0:T(8,128)S(...) conditional(s32[]{:T(128)} %bitcast.1, ...), branch_computations={%region_0.1_spmd, %region_1.2_spmd, %region_2.3_spmd, %region_3.4_... | conditional | bytes 802960 | solution.py:1005
  11.1 3.6 %collective-permute-start.1 = (f32[42,8,128]{2,1,0:T(8,128)S(1)}, f32[42,8,128]{2,1,0:T(8,128)S(1)}, u32[]{:S(2)}, u32[]{:S(2)}) collective-permute-start(f32[42,8,128]{2,1,0:T(8,128)S(1)} %get-tuple-element.76), channel_id=1, source_target_pairs={{2,2},{6,14},{10,10},{14,6},{3,3},{7,15},{11,11},{15,7},{18,18},{2... | collective-permute-start | bytes 516104 | tf_op jit(solution)/shard_map/cond/branch_0_fun/ppermute | solution.py:998
  14.6 0.1 collective-permute-start
  14.7 1.2 %edges.4 = (f32[3,128,128]{2,1,0:T(8,128)S(1)}, f32[128,128]{1,0:T(8,128)S(1)}, f32[5,3,128,128]{3,2,1,0:T(8,128)S(1)}) custom-call(f32[4,256,128]{2,1,0:T(8,128)S(1)} %get-tuple-element.62.own_ref.refs_1_, f32[28,8,128]{2,1,0:T(8,128)S(1)} %get-tuple-element.64.ra_ref, f32[28,8,128]{2,1,0:T(8,128)S(1)} %get-tuple-element.65.rb_ref), custom_call_target="tpu_custom_call" | custom-call | tf_op jit(solution)/shard_map/cond/branch_0_fun/jit(wrapped)/edges/pallas_call | solution.py:1000
  15.9 1.9 %wedge_rows.4 = (f32[3,320,128]{2,1,0:T(8,128)S(1)}, f32[3,320,128]{2,1,0:T(8,128)}, f32[320,128]{1,0:T(8,128)}, f32[4,160,128]{2,1,0:T(8,128)S(1)}, f32[3,128,1...) custom-call(f32[35,8,128]{2,1,0:T(8,128)S(1)} %get-tuple-element.61.refs_0_, ...), custom_call_target="tpu_custom_call" | custom-call | tf_op jit(solution)/shard_map/cond/branch_0_fun/jit(wrapped)/wedge_rows/pallas_call | solution.py:1001
  17.8 0.8 %collective-permute-done.refs_0_ = f32[7,8,128]{2,1,0:T(8,128)S(1)} collective-permute-done((f32[7,8,128]{2,1,0:T(8,128)S(1)}, f32[7,8,128]{2,1,0:T(8,128)S(1)}, u32[]{:S(2)}, u32[]{:S(2)}) %collective-permute-start) | collective-permute-done | bytes 28704 | tf_op jit(solution)/shard_map/cond/branch_0_fun/ppermute | solution.py:999
  18.6 1.1 %wedge_edges.4 = (f32[3,8,32,128]{3,2,1,0:T(8,128)S(1)}, f32[8,128]{1,0:T(8,128)S(1)}) custom-call(f32[7,8,128]{2,1,0:T(8,128)S(1)} %collective-permute-done.refs_0_, f32[5,3,256,128]{3,2,1,0:T(8,128)S(1)} %get-tuple-element.63.refs_2_.refs_1_, f32[3,320,128]{2,1,0:T(8,128)S(1)} %get-tuple-element.73.refs_2_, f32[4,160,128]{2,1,0:T(8,128)S(1)} %get-tuple-element.74.refs_3_, ...), custom_call_target="tpu_custom_call" | custom-call | tf_op jit(solution)/shard_map/cond/branch_0_fun/jit(wrapped)/wedge_edges/pallas_call | solution.py:1002
  19.6 0.0 collective-permute-done.1.fold_ref
  19.6 0.3 %north.4 = (f32[3,320,128]{2,1,0:T(8,128)S(1)}, f32[320,128]{1,0:T(8,128)S(1)}, f32[4,160,128]{2,1,0:T(8,128)S(1)}, f32[80,128]{1,0:T(8,128)S(1)}) custom-call(f32[42,8,128]{2,1,0:T(8,128)S(1)} %collective-permute-done.1.fold_ref, f32[8,128]{1,0:T(8,128)S(1)} %get-tuple-element.77.order_ref), custom_call_target="tpu_custom_call" | custom-call | tf_op jit(solution)/shard_map/cond/branch_0_fun/jit(wrapped)/north/pallas_call | solution.py:1003
  20.0 1.9 %last.1 = f32[3,8,32,128]{3,2,1,0:T(8,128)} custom-call(f32[3,8,32,128]{3,2,1,0:T(8,128)S(1)} %get-tuple-element.171.refs_0_, f32[4,256,128]{2,1,0:T(8,128)S(1)} %get-tuple-element.162.own_ref.refs_1_, f32[5,3,256,128]{3,2,1,0:T(8,128)S(1)} %get-tuple-element.167.refs_2_, f32[3,128,128]{2,1,0:T(8,128)S(1)} %get-tuple-element.172.refs_3_, ...), custom_call_target="tpu_custom_call" | custom-call | tf_op jit(solution)/shard_map/last/pallas_call | solution.py:1016
Async XLA Ops:
  1.6 9.5 %collective-permute-start.10 = (f32[35,8,128]{2,1,0:T(8,128)S(1)}, f32[35,8,128]{2,1,0:T(8,128)S(1)}, u32[]{:S(2)}, u32[]{:S(2)}) collective-permute-start(f32[35,8,128]{2,1,0:T(8,128)S(1)} %get-tuple-element.166), channel_id=1, source_target_pairs={{0,2},{2,0},{1,3},{3,1},{4,6},{6,4},{5,7},{7,5},{8,10},{10,8},{9,1... | collective-permute-start | bytes 430088 | tf_op jit(solution)/shard_map/ppermute | solution.py:934
  2.2 5.3 %collective-permute-start.8 = (f32[28,8,128]{2,1,0:T(8,128)S(1)}, f32[28,8,128]{2,1,0:T(8,128)S(1)}, u32[]{:S(2)}, u32[]{:S(2)}) collective-permute-start(f32[28,8,128]{2,1,0:T(8,128)S(1)} %get-tuple-element.164), channel_id=1, source_target_pairs={{0,4},{4,0},{8,12},{12,8},{1,5},{5,1},{9,13},{13,9},{2,6},{6,2},{1... | collective-permute-start | bytes 344072 | tf_op jit(solution)/shard_map/ppermute | solution.py:915
  2.2 8.2 %collective-permute-start.9 = (f32[28,8,128]{2,1,0:T(8,128)S(1)}, f32[28,8,128]{2,1,0:T(8,128)S(1)}, u32[]{:S(2)}, u32[]{:S(2)}) collective-permute-start(f32[28,8,128]{2,1,0:T(8,128)S(1)} %get-tuple-element.165), channel_id=1, source_target_pairs={{0,12},{4,8},{8,4},{12,0},{1,13},{5,9},{9,5},{13,1},{2,14},{6,10},... | collective-permute-start | bytes 344072 | tf_op jit(solution)/shard_map/ppermute | solution.py:915
  11.1 8.6 %collective-permute-start.1 = (f32[42,8,128]{2,1,0:T(8,128)S(1)}, f32[42,8,128]{2,1,0:T(8,128)S(1)}, u32[]{:S(2)}, u32[]{:S(2)}) collective-permute-start(f32[42,8,128]{2,1,0:T(8,128)S(1)} %get-tuple-element.76), channel_id=1, source_target_pairs={{2,2},{6,14},{10,10},{14,6},{3,3},{7,15},{11,11},{15,7},{18,18},{2... | collective-permute-start | bytes 516104 | tf_op jit(solution)/shard_map/cond/branch_0_fun/ppermute | solution.py:998
  14.6 3.9 %collective-permute-start = (f32[7,8,128]{2,1,0:T(8,128)S(1)}, f32[7,8,128]{2,1,0:T(8,128)S(1)}, u32[]{:S(2)}, u32[]{:S(2)}) collective-permute-start(f32[7,8,128]{2,1,0:T(8,128)S(1)} %get-tuple-element.72), channel_id=1, source_target_pairs={{0,2},{2,0},{1,3},{3,1},{4,6},{6,4},{5,7},{7,5},{8,10},{10,8},{9,1... | collective-permute-start | bytes 86024 | tf_op jit(solution)/shard_map/cond/branch_0_fun/ppermute | solution.py:999
